TPU v7x, 256 devices: a whole 4x4x8 slice. The times are simulated.
256 devices in a mesh: seq: 16 (over z, core), fft: 16 (over y, x).
Axes of the slice: x: 4, y: 4, z: 8, core: 2. Of those that a mesh axis runs over, the one named last changes fastest.
Arguments:
- projections: bfloat16 [3, 8192, 4096], P(None, 'seq', 'fft'), may hold values from -6 to 6
- taps: float32 [7, 3, 4096], P(None, None, 'fft'), may hold values from -2 to 2
- rates: float32 [4096, 16], replicated, may hold values from 6.1035156e-05 to 0.03
- residues: float32 [4096, 16], replicated, may hold values from -1 to 1
- skip: float32 [4096], P('fft'), may hold values from -2 to 2
Outputs:
- mixed: bfloat16 [8192, 4096], P('seq', 'fft')
All inputs are finite; a program needn't handle non-finite values.
Results may differ from a plain program's by a relative error of at most 0.007.
Values may be sent and summed in bfloat16 or wider, within the bound.
No kernel may reach another device: no remote copies, remote signals or barrier semaphores. Data moves between devices by JAX's collectives and lax.ppermute only.
A program may use at most 128 MiB of HBM per device.

v0:
```python
import math

import jax
import jax.numpy as jnp
from jax import lax
from jax.sharding import PartitionSpec as P


def passed_along(block, axis, distance):
    devices = range(lax.axis_size(axis))
    route = [(i - distance, i) for i in devices if i - distance in devices]
    return lax.ppermute(block, axis, route)


def complex_times(factor_one, factor_two):
    real_part = factor_one[0] * factor_two[0] - factor_one[1] * factor_two[1]
    imag_part = factor_one[0] * factor_two[1] + factor_one[1] * factor_two[0]
    return jnp.stack([real_part, imag_part])


def rotate(values, rotation):
    cosine = jnp.cos(rotation)
    sine = jnp.sin(rotation)
    return jnp.stack([values[0] * cosine - values[1] * sine, values[0] * sine + values[1] * cosine])


def dft_rows(count, direction):
    counter = jnp.arange(count, dtype=jnp.int32)
    product = counter[:, None] * counter[None, :] % count
    rotation = product.astype(jnp.float32) * (direction * 2.0 * math.pi / count)
    return jnp.stack([jnp.cos(rotation), jnp.sin(rotation)])


def mix_along(matrix, values, pattern):
    highest = lax.Precision.HIGHEST
    real_part = jnp.einsum(pattern, matrix[0], values[0], precision=highest) - jnp.einsum(
        pattern, matrix[1], values[1], precision=highest
    )
    imag_part = jnp.einsum(pattern, matrix[0], values[1], precision=highest) + jnp.einsum(
        pattern, matrix[1], values[0], precision=highest
    )
    return jnp.stack([real_part, imag_part])


def twiddle_angle(outer_len, inner_len, direction):
    outer_index = jnp.arange(outer_len, dtype=jnp.int32)[:, None]
    inner_index = jnp.arange(inner_len, dtype=jnp.int32)[None, :]
    product = outer_index * inner_index % (outer_len * inner_len)
    return product.astype(jnp.float32) * (direction * 2.0 * math.pi / (outer_len * inner_len))


def local_forward(signal, outer_len, inner_len):
    reim_count, row_count, channels, length = signal.shape
    blocks = signal.reshape(reim_count, row_count, channels, outer_len, inner_len)
    blocks = mix_along(dft_rows(outer_len, -1.0), blocks, "ac,rkab->rkcb")
    blocks = rotate(blocks, twiddle_angle(outer_len, inner_len, -1.0)[None, None, :, :])
    return mix_along(dft_rows(inner_len, -1.0), blocks, "bd,rkcb->rkcd")


def local_inverse(spectrum, outer_len, inner_len):
    reim_count, row_count, channels = (spectrum.shape[0], spectrum.shape[1], spectrum.shape[2])
    blocks = mix_along(dft_rows(inner_len, 1.0), spectrum, "db,rkcd->rkcb")
    blocks = rotate(blocks, twiddle_angle(outer_len, inner_len, 1.0)[None, None, :, :])
    blocks = mix_along(dft_rows(outer_len, 1.0), blocks, "ca,rkcb->rkab")
    return blocks.reshape(reim_count, row_count, channels, outer_len * inner_len)


def filter_spectrum(rates_own, residues_own, k_first, stride, outer_len, inner_len, full_len):
    outer_index = jnp.arange(outer_len, dtype=jnp.int32)[:, None]
    inner_index = jnp.arange(inner_len, dtype=jnp.int32)[None, :]
    k_second = outer_index + outer_len * inner_index
    frequency = k_first[:, None, None] + stride * k_second[None, :, :]
    theta = frequency.astype(jnp.float32)[:, None, :, :] * (2.0 * math.pi / full_len)
    half_sine = jnp.sin(0.5 * theta)
    full_sine = jnp.sin(theta)
    flip_sign = jnp.array([1.0, -1.0], jnp.float32)[:, None, None, None]
    seq_count = float(full_len // 2)
    rates_rows = rates_own.T
    residues_rows = residues_own.T
    channels = rates_own.shape[0]
    initial = jnp.zeros((2, channels, outer_len, inner_len), jnp.float32)

    def add_mode(mode_index, carried):
        spec_real, spec_imag = carried
        rate_now = lax.dynamic_index_in_dim(rates_rows, mode_index, 0, keepdims=False)[
            :, None, None
        ]
        residue_now = lax.dynamic_index_in_dim(residues_rows, mode_index, 0, keepdims=False)[
            :, None, None
        ]
        decay_now = jnp.exp(-rate_now)
        one_minus = -jnp.expm1(-rate_now)
        scale_now = residue_now * jnp.sqrt(-jnp.expm1(-2.0 * rate_now))
        tail_weight = jnp.exp(-rate_now * seq_count)
        numerator = scale_now * (1.0 - tail_weight * flip_sign)
        denom_real = one_minus + 2.0 * decay_now * half_sine * half_sine
        denom_imag = decay_now * full_sine
        weight_now = numerator / (denom_real * denom_real + denom_imag * denom_imag)
        return (spec_real + weight_now * denom_real, spec_imag - weight_now * denom_imag)

    spec_real, spec_imag = lax.fori_loop(0, rates_own.shape[1], add_mode, (initial, initial))
    return jnp.stack([spec_real, spec_imag])


def transform_convolve(owned_rows, rates_own, residues_own):
    channels, length = owned_rows.shape
    full_len = 2 * length
    signal = owned_rows.astype(jnp.float32)
    zero_field = jnp.zeros_like(signal)
    values = jnp.stack([jnp.stack([signal, signal]), jnp.stack([zero_field, zero_field])])
    k_first = jnp.arange(2, dtype=jnp.int32)
    positions = jnp.arange(length, dtype=jnp.int32)
    row_phase = (positions[None, :] * k_first[:, None] % full_len).astype(jnp.float32) * (
        -2.0 * math.pi / full_len
    )
    values = rotate(values, row_phase[:, None, :])
    inner_len = math.gcd(length, 128)
    outer_len = length // inner_len
    spectrum = local_forward(values, outer_len, inner_len)
    response = filter_spectrum(rates_own, residues_own, k_first, 2, outer_len, inner_len, full_len)
    spectrum = complex_times(spectrum, response)
    values = local_inverse(spectrum, outer_len, inner_len)
    values = rotate(values, -row_phase[:, None, :])
    combined = values[0, 0] + values[0, 1]
    return combined * (1.0 / full_len)


def long_convolution(gated_input, rates, residues):
    seq_count = lax.axis_size("seq")
    fft_count = lax.axis_size("fft")
    seq_index = lax.axis_index("seq")
    fft_index = lax.axis_index("fft")
    tok_rows, local_channels = gated_input.shape
    mode_count = rates.shape[1]
    group_width = local_channels // seq_count
    rates_grid = lax.dynamic_index_in_dim(
        rates.reshape(fft_count, seq_count, group_width, mode_count), seq_index, 1, keepdims=False
    )
    residues_grid = lax.dynamic_index_in_dim(
        residues.reshape(fft_count, seq_count, group_width, mode_count),
        seq_index,
        1,
        keepdims=False,
    )
    owned_rows = lax.all_to_all(gated_input.T, "seq", split_axis=0, concat_axis=1, tiled=True)
    rates_own = lax.dynamic_index_in_dim(rates_grid, fft_index, 0, keepdims=False)
    residues_own = lax.dynamic_index_in_dim(residues_grid, fft_index, 0, keepdims=False)
    result = transform_convolve(owned_rows, rates_own, residues_own)
    home_rows = lax.all_to_all(
        result.astype(jnp.bfloat16), "seq", split_axis=1, concat_axis=0, tiled=True
    )
    return home_rows.T


def on_device(projections, taps, rates, residues, skip):
    tap_count = taps.shape[0]
    tok_rows = projections.shape[1]
    causal_rows = passed_along(projections[:, tok_rows - (tap_count - 1) :, :], "seq", 1)
    extended = jnp.concatenate([causal_rows, projections], axis=1)
    filtered = jnp.zeros(projections.shape, jnp.float32)
    for offset in range(tap_count):
        begin_row = tap_count - 1 - offset
        filtered = filtered + taps[offset][:, None, :] * extended[
            :, begin_row : begin_row + tok_rows, :
        ].astype(jnp.float32)
    gated_input = (filtered[1] * filtered[2]).astype(jnp.bfloat16)
    long_out = long_convolution(gated_input, rates, residues)
    mixed = filtered[0] * (
        long_out.astype(jnp.float32) + skip[None, :] * gated_input.astype(jnp.float32)
    )
    return mixed.astype(jnp.bfloat16)


def solution(mesh):
    in_specs = (P(None, "seq", "fft"), P(None, None, "fft"), P(), P(), P("fft"))
    out_specs = P("seq", "fft")
    return jax.shard_map(
        on_device, mesh=mesh, in_specs=in_specs, out_specs=out_specs, check_vma=False
    )
```

profile of v0, /device:TPU:1, one launch (start us, length us, event | category | flops | bytes accessed | tf_op | source)
XLA Modules:
  0.0 106.4 jit_solution(6087864838606859630)
XLA Ops:
  0.9 4.9 %collective-permute-start = (bf16[3,6,256]{1,2,0:T(8,128)(2,1)S(1)}, bf16[3,6,256]{1,2,0:T(8,128)(2,1)S(1)}, u32[]{:S(2)}, u32[]{:S(2)}) collective-permute-start(bf16[3,6,256]{1,2,0:T(8,128)(2,1)S(1)} %copy.26), channel_id=1, source_target_pairs={{0,16},{16,32},{32,48},{48,64},{64,80},{80,96},{96,112},{112,128},... | collective-permute-start | bytes 27656 | tf_op jit(solution)/shard_map/ppermute | solution.py:12
  8.0 3.0 %reshape.413 = f32[16,16,16,16]{2,1,0,3:T(8,128)} reshape(f32[4096,16]{0,1:T(8,128)} %param.10) | data formatting | bytes 524288 | tf_op jit(solution)/shard_map/reshape | solution.py:137
  11.0 2.0 %reshape.412 = f32[16,16,16,16]{2,1,0,3:T(8,128)} reshape(f32[4096,16]{0,1:T(8,128)S(1)} %copy-done.2) | data formatting | bytes 524288 | tf_op jit(solution)/shard_map/reshape | solution.py:140
  14.0 22.1 %while.19 = (s32[]{:T(128)}, f32[2,16,64,128]{3,2,1,0:T(8,128)S(1)}, f32[2,16,64,128]{3,2,1,0:T(8,128)S(1)}, f32[16,16]{1,0:T(8,128)S(1)}, f32[16,16]{1,0:T(8,12...) while((s32[]{:T(128)}, ...), condition=%wide.region_1.2_spmd.clone.clone.clone.clone, body=%wide.region_0.1_spmd.clone.clone.clone.clone.sunk | while | flops 3735763 | bytes 4490555 | solution.py:101
  36.3 1.4 %copy.25 = bf16[3,512,256]{1,2,0:T(8,128)(2,1)S(1)} copy(bf16[3,512,256]{2,1,0:T(8,128)(2,1)} %param.8) | data formatting | bytes 1572864 | tf_op args[0]
  37.7 2.9 %multiply_add_fusion.1 = f32[3,512,256]{1,2,0:T(8,128)S(1)} fusion(bf16[3,512,256]{1,2,0:T(8,128)(2,1)S(1)} %copy.25, bf16[3,6,256]{1,2,0:T(8,128)(2,1)S(1)} %collective-permute-done, f32[3,256]{1,0:T(4,128)S(1)} %get-tuple-element.270, f32[3,256]{1,0:T(4,128)S(1)} %get-tuple-element.271, f32[3,256]{1,0:T(4,128)S(1)} %get-tuple-element.272, ...), kind=kLoop, calls=%fused_computation.26 | loop fusion | flops 14942208 | bytes 2390016 | tf_op jit(solution)/shard_map/add | solution.py:163
  42.6 7.7 %all-to-all-start = ((bf16[16,16,512]{2,1,0:T(8,128)(2,1)}), bf16[16,16,512]{2,1,0:T(8,128)(2,1)S(1)}, u32[]{:S(2)}, u32[]{:S(2)}) async-start(bf16[16,16,512]{2,1,0:T(8,128)(2,1)} %bitcast.3), calls=%async_computation | async-start | bytes 524288 | tf_op jit(solution)/shard_map/all_to_all | solution.py:145
  50.9 11.1 %all-to-all-done = bf16[16,16,512]{2,1,0:T(8,128)(2,1)S(1)} async-done(((bf16[16,16,512]{2,1,0:T(8,128)(2,1)}), bf16[16,16,512]{2,1,0:T(8,128)(2,1)S(1)}, u32[]{:S(2)}, u32[]{:S(2)}) %all-to-all-start) | async-done | bytes 262176 | tf_op jit(solution)/shard_map/all_to_all | solution.py:145
  62.3 1.3 %fusion.19 = f32[2,16,128,64]{2,3,1,0:T(8,128)S(1)} fusion(f32[2,64,128]{2,1,0:T(8,128)S(1)} %cosine_multiply_fusion, f32[2,64,128]{2,1,0:T(8,128)S(1)} %get-tuple-element.262, bf16[1,16,64,128]{3,2,1,0:T(8,128)(2,1)S(1)} %convert_element_type.192), kind=kOutput, calls=%fused_computation.44 | convolution fusion | flops 202432512 | bytes 1441792 | tf_op jit(solution)/shard_map/ac,rkab->rkcb/dot_general | solution.py:39
  63.6 1.3 %fusion.16 = f32[2,16,128,64]{2,3,1,0:T(8,128)S(1)} fusion(f32[2,64,128]{2,1,0:T(8,128)S(1)} %get-tuple-element.278, f32[2,64,128]{2,1,0:T(8,128)S(1)} %get-tuple-element.261, bf16[1,16,64,128]{3,2,1,0:T(8,128)(2,1)S(1)} %convert_element_type.192), kind=kOutput, calls=%fused_computation.42 | convolution fusion | flops 202432512 | bytes 1441792 | tf_op jit(solution)/shard_map/ac,rkab->rkcb/dot_general | solution.py:36
  64.9 1.4 %fusion.12 = f32[2,16,64,128]{3,2,1,0:T(8,128)S(1)} fusion(f32[2,16,128,64]{2,3,1,0:T(8,128)S(1)} %fusion.19, f32[2,64,128]{2,1,0:T(8,128)S(1)} %get-tuple-element.278, f32[2,64,128]{2,1,0:T(8,128)S(1)} %get-tuple-element.261, bf16[1,16,64,128]{3,2,1,0:T(8,128)(2,1)S(1)} %convert_element_type.192), kind=kOutput, calls=%fused_computation.36 | convolution fusion | flops 202694656 | bytes 2490368 | tf_op jit(solution)/shard_map/ac,rkab->rkcb/dot_general | solution.py:39
  66.3 1.4 %fusion.13 = f32[2,16,64,128]{3,2,1,0:T(8,128)S(1)} fusion(f32[2,16,128,64]{2,3,1,0:T(8,128)S(1)} %fusion.16, f32[2,64,128]{2,1,0:T(8,128)S(1)} %cosine_multiply_fusion, f32[2,64,128]{2,1,0:T(8,128)S(1)} %get-tuple-element.262, bf16[1,16,64,128]{3,2,1,0:T(8,128)(2,1)S(1)} %convert_element_type.192), kind=kOutput, calls=%fused_computation.38 | convolution fusion | flops 202694656 | bytes 2490368 | tf_op jit(solution)/shard_map/ac,rkab->rkcb/dot_general | solution.py:36
  67.7 1.2 %fusion.40 = f32[2,16,64,128]{3,2,1,0:T(8,128)S(1)} fusion(f32[2,16,64,128]{3,2,1,0:T(8,128)S(1)} %fusion.12, f32[2,16,64,128]{3,2,1,0:T(8,128)S(1)} %fusion.13, f32[64,128]{1,0:T(8,128)S(1)} %get-tuple-element.279, f32[64,128]{1,0:T(8,128)S(1)} %get-tuple-element.280), kind=kOutput, calls=%fused_computation.81 | convolution fusion | flops 403668992 | bytes 3211264 | tf_op jit(solution)/shard_map/bd,rkcb->rkcd/dot_general | solution.py:36
  68.9 1.2 %fusion.41 = f32[2,16,64,128]{3,2,1,0:T(8,128)S(1)} fusion(f32[2,16,64,128]{3,2,1,0:T(8,128)S(1)} %fusion.12, f32[2,16,64,128]{3,2,1,0:T(8,128)S(1)} %fusion.13, f32[64,128]{1,0:T(8,128)S(1)} %get-tuple-element.279, f32[64,128]{1,0:T(8,128)S(1)} %get-tuple-element.280), kind=kOutput, calls=%fused_computation.82 | convolution fusion | flops 403668992 | bytes 3211264 | tf_op jit(solution)/shard_map/bd,rkcb->rkcd/dot_general | solution.py:39
  70.2 1.2 %convolution_subtract_fusion.2 = f32[2,16,64,128]{3,2,1,0:T(8,128)S(1)} fusion(f32[2,16,64,128]{3,2,1,0:T(8,128)S(1)} %fusion.40, f32[2,16,64,128]{3,2,1,0:T(8,128)S(1)} %fusion.12, f32[2,16,64,128]{3,2,1,0:T(8,128)S(1)} %fusion.13, f32[64,128]{1,0:T(8,128)S(1)} %get-tuple-element.279, f32[64,128]{1,0:T(8,128)S(1)} %get-tuple-element.280), kind=kOutput, calls=%fused_computation.34 | convolution fusion | flops 403931136 | bytes 4259840 | tf_op jit(solution)/shard_map/bd,rkcb->rkcd/dot_general | solution.py:36
  71.5 1.5 %multiply_subtract_fusion.2 = (f32[2,16,64,128]{3,2,1,0:T(8,128)S(1)}, f32[2,16,64,128]{3,2,1,0:T(8,128)S(1)}) fusion(f32[2,16,64,128]{3,2,1,0:T(8,128)S(1)} %get-tuple-element.149, f32[2,16,64,128]{3,2,1,0:T(8,128)S(1)} %convolution_subtract_fusion.2, f32[2,16,64,128]{3,2,1,0:T(8,128)S(1)} %get-tuple-element.148, f32[2,16,64,128]{3,2,1,0:T(8,128)S(1)} %fusion.41, ...), kind=kOutput, calls=%fused_computation.49 | convolution fusion | flops 405504000 | bytes 8454144 | tf_op jit(solution)/shard_map/bd,rkcb->rkcd/dot_general | solution.py:39
  72.9 1.5 %fusion.58 = f32[2,16,64,128]{3,2,1,0:T(8,128)S(1)} fusion(f32[2,16,64,128]{3,2,1,0:T(8,128)S(1)} %get-tuple-element.260), kind=kOutput, calls=%fused_computation.111 | convolution fusion | flops 402882560 | bytes 2097152 | tf_op jit(solution)/shard_map/db,rkcd->rkcb/dot_general | solution.py:39
  78.1 1.3 %fusion.43 = f32[2,16,128,64]{2,3,1,0:T(8,128)S(1)} fusion(f32[2,16,64,128]{3,2,1,0:T(8,128)S(1)} %convolution_add_fusion.1, f32[2,16,64,128]{3,2,1,0:T(8,128)S(1)} %convolution_subtract_fusion.1, f32[64,128]{1,0:T(8,128)S(1)} %get-tuple-element.281, f32[64,128]{1,0:T(8,128)S(1)} %get-tuple-element.282), kind=kOutput, calls=%fused_computation.84 | convolution fusion | flops 202170368 | bytes 3211264 | tf_op jit(solution)/shard_map/ca,rkcb->rkab/dot_general | solution.py:39
  79.4 2.3 %fusion.42 = f32[2,16,128,64]{2,3,1,0:T(8,128)} fusion(f32[2,16,64,128]{3,2,1,0:T(8,128)S(1)} %convolution_add_fusion.1, f32[2,16,64,128]{3,2,1,0:T(8,128)S(1)} %convolution_subtract_fusion.1, f32[64,128]{1,0:T(8,128)S(1)} %get-tuple-element.281, f32[64,128]{1,0:T(8,128)S(1)} %get-tuple-element.282), kind=kOutput, calls=%fused_computation.83 | convolution fusion | flops 202170368 | bytes 3211264 | tf_op jit(solution)/shard_map/ca,rkcb->rkab/dot_general | solution.py:36
  81.7 2.3 %fusion.10 = f32[2,16,64,128]{3,2,1,0:T(8,128)} fusion(f32[2,16,128,64]{2,3,1,0:T(8,128)S(1)} %fusion.43, f32[2,16,64,128]{3,2,1,0:T(8,128)S(1)} %convolution_add_fusion.1, f32[2,16,64,128]{3,2,1,0:T(8,128)S(1)} %convolution_subtract_fusion.1, f32[64,128]{1,0:T(8,128)S(1)} %get-tuple-element.281, f32[64,128]{1,0:T(8,128)S(1)} %get-tuple-element.282), kind=kOutput, calls=%fused_computation.28 | convolution fusion | flops 202432512 | bytes 4259840 | tf_op jit(solution)/shard_map/ca,rkcb->rkab/dot_general | solution.py:39
  84.0 1.4 %squeeze.38 = f32[1,2,16,8192]{3,2,1,0:T(8,128)S(1)} reshape(f32[2,16,64,128]{3,2,1,0:T(8,128)} %fusion.10) | data formatting | bytes 2097152 | tf_op jit(solution)/shard_map/squeeze | solution.py:24
  85.4 3.5 %fusion.11 = f32[2,16,64,128]{3,2,1,0:T(8,128)} fusion(f32[2,16,128,64]{2,3,1,0:T(8,128)} %fusion.42, f32[2,16,64,128]{3,2,1,0:T(8,128)S(1)} %convolution_add_fusion.1, f32[2,16,64,128]{3,2,1,0:T(8,128)S(1)} %convolution_subtract_fusion.1, f32[64,128]{1,0:T(8,128)S(1)} %get-tuple-element.281, f32[64,128]{1,0:T(8,128)S(1)} %get-tuple-element.282), kind=kOutput, calls=%fused_computation.30 | convolution fusion | flops 202432512 | bytes 4259840 | tf_op jit(solution)/shard_map/ca,rkcb->rkab/dot_general | solution.py:36
  88.9 1.4 %squeeze.37 = f32[1,2,16,8192]{3,2,1,0:T(8,128)S(1)} reshape(f32[2,16,64,128]{3,2,1,0:T(8,128)} %fusion.11) | data formatting | bytes 2097152 | tf_op jit(solution)/shard_map/squeeze | solution.py:24
  90.8 14.6 %all_to_all.23 = bf16[16,16,512]{2,0,1:T(8,128)(2,1)S(1)} all-to-all(bf16[16,16,512]{2,0,1:T(8,128)(2,1)S(1)} %copy.31), channel_id=1, replica_groups=mesh['seq'=16,'fft'=16] {'seq'}, dimensions={1} | all-to-all | bytes 524288 | tf_op jit(solution)/shard_map/all_to_all | solution.py:149
  (137 shorter events, 33.4 us)
Async XLA Ops:
  0.0 11.0 %copy-start.2 = (f32[4096,16]{0,1:T(8,128)S(1)}, f32[4096,16]{0,1:T(8,128)}, u32[]{:S(2)}) copy-start(f32[4096,16]{0,1:T(8,128)} %param.11) | copy-start | bytes 786436
  0.9 36.8 %collective-permute-start = (bf16[3,6,256]{1,2,0:T(8,128)(2,1)S(1)}, bf16[3,6,256]{1,2,0:T(8,128)(2,1)S(1)}, u32[]{:S(2)}, u32[]{:S(2)}) collective-permute-start(bf16[3,6,256]{1,2,0:T(8,128)(2,1)S(1)} %copy.26), channel_id=1, source_target_pairs={{0,16},{16,32},{32,48},{48,64},{64,80},{80,96},{96,112},{112,128},... | collective-permute-start | bytes 27656 | tf_op jit(solution)/shard_map/ppermute | solution.py:12
  11.0 2.9 %copy-start.3 = (f32[2]{0:T(128)S(1)}, f32[2]{0:T(128)}, u32[]{:S(2)}) copy-start(f32[2]{0:T(128)} %constant.466) | copy-start | bytes 28
  40.6 1.2 %copy-start = (f32[3,512,256]{1,2,0:T(8,128)}, f32[3,512,256]{1,2,0:T(8,128)S(1)}, u32[]{:S(2)}) copy-start(f32[3,512,256]{1,2,0:T(8,128)S(1)} %multiply_add_fusion.1) | copy-start | bytes 4718596
  42.6 19.4 %all-to-all-start = ((bf16[16,16,512]{2,1,0:T(8,128)(2,1)}), bf16[16,16,512]{2,1,0:T(8,128)(2,1)S(1)}, u32[]{:S(2)}, u32[]{:S(2)}) async-start(bf16[16,16,512]{2,1,0:T(8,128)(2,1)} %bitcast.3), calls=%async_computation | async-start | bytes 524288 | tf_op jit(solution)/shard_map/all_to_all | solution.py:145
  90.5 14.9 %copy-start.1 = (f32[3,512,256]{1,2,0:T(8,128)S(1)}, f32[3,512,256]{1,2,0:T(8,128)}, u32[]{:S(2)}) copy-start(f32[3,512,256]{1,2,0:T(8,128)} %copy-done) | copy-start | bytes 4718596
  90.5 14.9 %copy-start.4 = (f32[256]{0:T(256)S(1)}, f32[256]{0:T(256)}, u32[]{:S(2)}) copy-start(f32[256]{0:T(256)} %param.12) | copy-start | bytes 3076
where the time goes:
time: 107 us; the launch traced here: 106 us
  other arithmetic  27.2 us (25%)
  matrix products  25.1 us (23%)
  local copies, waits for them, and re-layouts  14.7 us (14%)
  blocking collectives  14.6 us (14%)
  starting transfers between devices  12.6 us (12%)
  waiting for transfers between devices  11.1 us (10%)
    all_to_all x1, blocking collectives, long_convolution(): lax.all_to_all(result.astype(jnp.bfloat16), 'seq', split_axis=1, concat_a...  14.6 us
    sub x16, other arithmetic, add_mode(): spec_imag - weight_now * denom_imag  12.5 us
    all_to_all x1, waiting for transfers between devices, long_convolution(): lax.all_to_all(gated_input.T, 'seq', split_axis=0, concat_axis=1, tiled=T...  11.1 us
    all_to_all x1, starting transfers between devices, long_convolution(): lax.all_to_all(gated_input.T, 'seq', split_axis=0, concat_axis=1, tiled=T...  7.69 us
    dot_general x4, matrix products, mix_along(): jnp.einsum(pattern, matrix[1], values[1], precision=highest)  7.35 us
    mul x16, other arithmetic, add_mode(): denom_imag = decay_now * full_sine  7.03 us
    dot_general x4, matrix products, mix_along(): jnp.einsum(pattern, matrix[1], values[0], precision=highest)  6.36 us
    dot_general x4, matrix products, mix_along(): jnp.einsum(pattern, matrix[0], values[0], precision=highest)  6.06 us
  transfers between devices with their start and end apart: 2, of which 1 were waited for; matrix products, arithmetic and copies ran while one was open for 30% of the time, Pallas kernels for 0%

commit v1 on v0

v1 whole, which is shorter than its diff:
```python
import jax
import jax.numpy as jnp
from jax import lax
from jax.experimental import pallas as pl
from jax.experimental.pallas import tpu as pltpu
from jax.sharding import PartitionSpec as P

CHUNKS = 8
LANES = 128
PAD = 8


def rounded(values):
    return values.astype(jnp.bfloat16).astype(jnp.float32)


def spread(row):
    return jnp.broadcast_to(row, (CHUNKS, row.shape[-1]))


def pairwise_sum(terms):
    while len(terms) > 1:
        joined = [a + b for a, b in zip(terms[0::2], terms[1::2])]
        terms = joined + ([terms[-1]] if len(terms) % 2 else [])
    return terms[0]


def one_minus_exp(y):
    series = jnp.ones_like(y)
    for divisor in (7.0, 6.0, 5.0, 4.0, 3.0, 2.0):
        series = 1.0 - y * (1.0 / divisor) * series
    return jnp.where(y < 0.1, y * series, 1.0 - jnp.exp(-y))


def chunk_rows(buffer, first, count, stride):
    return [buffer[pl.ds(PAD + first + k, CHUNKS, stride=stride), :] for k in range(count)]


def filter_chunks(buffer, taps, length, emit):
    tap_count = len(taps)
    step = 8
    for first in range(0, length, step):
        rows = chunk_rows(buffer, first - (tap_count - 1), step + tap_count - 1, length)
        for k in range(step):
            terms = [taps[i] * rows[k + tap_count - 1 - i] for i in range(tap_count)]
            emit(first + k, pairwise_sum(terms))


def state_kernel(
    rates_hbm, residues_hbm, taps_ref, tokens_hbm, gated_ref, ends_ref, state_ref, head_ref, tail_ref, rates_ref, scale_ref,
    bits_ref, head_bits_ref, tail_bits_ref, residues_ref, one_ref, two_ref, sems,
):
    channels = rates_ref.shape[1]
    mode_count = rates_ref.shape[0]
    token_count = bits_ref.shape[2]
    length = token_count // CHUNKS
    tap_count = taps_ref.shape[1]
    halo_rows = tap_count - 1
    halves = channels // LANES
    edge_rows = head_bits_ref.shape[0]
    start = pl.multiple_of(lax.axis_index("fft") * channels, channels)
    loads = []
    for half in range(halves):
        for q in (1, 2):
            copy = pltpu.make_async_copy(
                tokens_hbm.at[q, :, pl.ds(half * LANES, LANES)], bits_ref.at[half, q - 1], sems.at[2 * half + q - 1]
            )
            copy.start()
            loads.append(copy)
    late = [
        pltpu.make_async_copy(rates_hbm.at[:, pl.ds(start, channels)], rates_ref, sems.at[2 * halves]),
        pltpu.make_async_copy(residues_hbm.at[:, pl.ds(start, channels)], residues_ref, sems.at[2 * halves + 1]),
        pltpu.make_async_copy(tokens_hbm.at[0, 0:edge_rows, :], head_bits_ref, sems.at[2 * halves + 2]),
        pltpu.make_async_copy(
            tokens_hbm.at[0, token_count - edge_rows : token_count, :], tail_bits_ref, sems.at[2 * halves + 3]
        ),
    ]
    for copy in late:
        copy.start()
    sublane = lax.broadcasted_iota(jnp.int32, (CHUNKS, LANES), 0)
    keep = jnp.where(sublane == 0, jnp.where(lax.axis_index("seq") == 0, 1.0, 0.0), 1.0)
    to_end = -((CHUNKS - 1 - sublane) * length).astype(jnp.float32)
    zero_rows = jnp.zeros((PAD, LANES), jnp.float32)
    for half in range(halves):
        lanes = slice(half * LANES, (half + 1) * LANES)
        for buffer, q in ((one_ref, 1), (two_ref, 2)):
            loads[2 * half + q - 1].wait()
            buffer[half, 0:PAD, :] = zero_rows
            buffer[half, PAD:, :] = bits_ref[half, q - 1].astype(jnp.float32)
            head_ref[q, :, lanes] = buffer[half, PAD : 2 * PAD, :]
            tail_ref[q, :, lanes] = buffer[half, token_count:, :]

        def emit_one(j, row):
            gated_ref[j, :, lanes] = row

        def emit_gate(j, row):
            gated = rounded(gated_ref[j, :, lanes] * row)
            if j < halo_rows:
                gated = gated * keep
            gated_ref[j, :, lanes] = gated

        filter_chunks(one_ref.at[half], [spread(taps_ref[1, i : i + 1, lanes]) for i in range(tap_count)], length, emit_one)
        filter_chunks(two_ref.at[half], [spread(taps_ref[2, i : i + 1, lanes]) for i in range(tap_count)], length, emit_gate)
        if half == 0:
            for copy in late:
                copy.wait()
            head_ref[0] = head_bits_ref[...].astype(jnp.float32)[:PAD]
            tail_ref[0] = tail_bits_ref[...].astype(jnp.float32)[edge_rows - PAD :]
            scale_ref[...] = residues_ref[...] * jnp.sqrt(one_minus_exp(2.0 * rates_ref[...]))
        rates = rates_ref[:, lanes]
        decay = jnp.exp(-rates)
        decays = [spread(decay[m : m + 1]) for m in range(mode_count)]
        states = [gated_ref[0, :, lanes]] * mode_count
        for j in range(1, length):
            row = gated_ref[j, :, lanes]
            states = [d * h + row for d, h in zip(decays, states)]
        for m in range(mode_count):
            ends_ref[m, :, lanes] = states[m]
            weight = jnp.exp(spread(rates[m : m + 1]) * to_end)
            state_ref[m : m + 1, lanes] = jnp.sum(weight * states[m], axis=0, keepdims=True)


def local_kernel(
    rates_ref, scale_ref, taps_ref, skip_ref, zeroth_ref, gated_ref, local_ref, gate_ref, skip_row_ref, buffer_ref
):
    length = zeroth_ref.shape[1] // CHUNKS
    mode_count = rates_ref.shape[0]
    tap_count = taps_ref.shape[1]
    skip_row_ref[...] = skip_ref[...]
    buffer_ref[0:PAD, :] = jnp.zeros((PAD, LANES), jnp.float32)
    buffer_ref[PAD:, :] = zeroth_ref[0].astype(jnp.float32)

    def emit(j, row):
        gate_ref[j] = row

    filter_chunks(buffer_ref, [spread(taps_ref[0, i : i + 1, :]) for i in range(tap_count)], length, emit)
    decay = jnp.exp(-rates_ref[...])
    decays = [spread(decay[m : m + 1]) for m in range(mode_count)]
    scales = [spread(scale_ref[m : m + 1, :]) for m in range(mode_count)]
    states = [gated_ref[0]] * mode_count
    for j in range(length):
        if j > 0:
            row = gated_ref[j]
            states = [d * h + row for d, h in zip(decays, states)]
        local_ref[j] = pairwise_sum([c * h for c, h in zip(scales, states)])


def final_kernel(
    rates_ref, scale_ref, taps_ref, skip_ref, incoming_ref, halo_ref, head_ref, ends_ref, gated_ref, local_ref,
    gate_ref, out_ref, edge_ref, rows_ref,
):
    length = gated_ref.shape[0]
    mode_count = rates_ref.shape[0]
    tap_count = taps_ref.shape[1]
    halo_rows = tap_count - 1
    sublane = lax.broadcasted_iota(jnp.int32, (CHUNKS, LANES), 0)
    edges = []
    for q in range(3):
        edge_ref[q, 0:PAD, :] = halo_ref[q]
        edge_ref[q, PAD : 2 * PAD, :] = head_ref[q, 0:PAD, :]
        edges.append(
            pairwise_sum([taps_ref[q, i : i + 1, :] * edge_ref[q, PAD - i : 2 * PAD - i, :] for i in range(tap_count)])
        )
    edge_gated = rounded(edges[1] * edges[2]) * jnp.where(lax.axis_index("seq") == 0, 0.0, 1.0)
    rates = rates_ref[...]
    scale = scale_ref[...]
    decay = jnp.exp(-rates)
    edge_state = jnp.zeros_like(decay)
    for t in range(halo_rows):
        edge_state = decay * edge_state + edge_gated[t : t + 1]
    edge_state = edge_state * jnp.exp(-rates * float(length - halo_rows))
    chunk_decay = jnp.exp(-rates * float(length))
    decays = [spread(decay[m : m + 1]) for m in range(mode_count)]
    states = []
    for m in range(mode_count):
        factor = spread(chunk_decay[m : m + 1])
        ends = ends_ref[m] + jnp.where(sublane == 0, spread(edge_state[m : m + 1]), 0.0)
        carried = jnp.where(sublane == 0, spread(incoming_ref[m : m + 1, :]), pltpu.roll(ends, 1, 0))
        for distance in (1, 2, 4):
            carried = carried + jnp.where(sublane >= distance, factor * pltpu.roll(carried, distance, 0), 0.0)
            factor = factor * factor
        states.append(carried * spread(scale[m : m + 1]))
    skip = spread(skip_ref[...])
    for j in range(length):
        states = [d * h for d, h in zip(decays, states)]
        gated, gate = gated_ref[j], gate_ref[j]
        if j < halo_rows:
            new = jnp.where(sublane == 0, spread(edge_gated[j : j + 1]), 0.0)
            states = [h + spread(scale[m : m + 1]) * new for m, h in enumerate(states)]
            gated = gated + new
            gate = jnp.where(sublane == 0, spread(edges[0][j : j + 1]), gate)
        long_out = rounded(local_ref[j] + pairwise_sum(states))
        rows_ref[pl.ds(j, CHUNKS, stride=length), :] = gate * (long_out + skip * gated)
    out_ref[...] = rows_ref[...].astype(jnp.bfloat16)


def by_lanes(*dims):
    return pl.BlockSpec((*dims, LANES), lambda i: (*(0 for _ in dims), i))


def one_projection(q, tokens):
    return pl.BlockSpec((1, tokens, LANES), lambda i: (q, 0, i))


def shape32(*dims):
    return jax.ShapeDtypeStruct(dims, jnp.float32)


PARAMS = pltpu.CompilerParams(vmem_limit_bytes=24 * 1024 * 1024)


def on_device(projections, taps, rates, residues, skip):
    tap_count = taps.shape[0]
    halo_rows = tap_count - 1
    _, tokens, channels = projections.shape
    mode_count = rates.shape[1]
    length = tokens // CHUNKS
    grid = (channels // LANES,)
    halves = channels // LANES
    count = lax.axis_size("seq")
    index = lax.axis_index("seq")
    taps = taps.transpose(1, 0, 2)
    hbm = pl.BlockSpec(memory_space=pltpu.HBM)
    vmem = pl.BlockSpec(memory_space=pltpu.VMEM)
    gated, ends, state, head, tail, rates_own, scale = pl.pallas_call(
        state_kernel,
        out_shape=(
            shape32(length, CHUNKS, channels),
            shape32(mode_count, CHUNKS, channels),
            shape32(mode_count, channels),
            shape32(3, PAD, channels),
            shape32(3, PAD, channels),
            shape32(mode_count, channels),
            shape32(mode_count, channels),
        ),
        in_specs=[hbm, hbm, vmem, hbm],
        out_specs=(vmem,) * 7,
        scratch_shapes=[
            pltpu.VMEM((halves, 2, tokens, LANES), jnp.bfloat16),
            pltpu.VMEM((2 * PAD, channels), jnp.bfloat16),
            pltpu.VMEM((2 * PAD, channels), jnp.bfloat16),
            pltpu.VMEM((mode_count, channels), jnp.float32),
            pltpu.VMEM((halves, PAD + tokens, LANES), jnp.float32),
            pltpu.VMEM((halves, PAD + tokens, LANES), jnp.float32),
            pltpu.SemaphoreType.DMA((2 * halves + 4,)),
        ],
        compiler_params=PARAMS,
        name="state",
    )(*(pltpu.with_memory_space_constraint(array, pltpu.HBM) for array in (rates.T, residues.T)), taps,
      pltpu.with_memory_space_constraint(projections, pltpu.HBM))
    taps_spec = by_lanes(3, tap_count)
    modes_spec = by_lanes(mode_count)
    grid_spec = by_lanes(length, CHUNKS)
    ends_spec = by_lanes(mode_count, CHUNKS)
    local, gate, skip_row = pl.pallas_call(
        local_kernel,
        out_shape=(shape32(length, CHUNKS, channels),) * 2 + (shape32(1, channels),),
        grid=grid,
        in_specs=[modes_spec, modes_spec, taps_spec, by_lanes(1), one_projection(0, tokens), grid_spec],
        out_specs=(grid_spec, grid_spec, by_lanes(1)),
        scratch_shapes=[pltpu.VMEM((PAD + tokens, LANES), jnp.float32)],
        compiler_params=PARAMS,
        name="local",
    )(rates_own, scale, taps, skip[None, :], projections, gated)

    def decayed(steps):
        return jnp.exp(-rates_own * jnp.asarray(steps, jnp.float32))

    def exchange(state, first, last, flip):
        high = lax.reduce_precision(state, 8, 7)
        rows = [high, state - high, last.reshape(3 * PAD, channels), first.reshape(2 * PAD, channels)]
        packed = jnp.concatenate(rows, axis=0).astype(jnp.bfloat16)
        packed = lax.ppermute(packed, "seq", [(i, i ^ flip) for i in range(count)]).astype(jnp.float32)
        edges = packed[2 * mode_count :].reshape(5, PAD, channels)
        return packed[:mode_count] + packed[mode_count : 2 * mode_count], edges[3:], edges[:3]

    halo = jnp.zeros_like(tail)
    prefix = jnp.zeros_like(state)
    first, last = head[1:], tail
    size = 1
    while size < count:
        flip = {1: 1, 2: 3, 4: 5, 8: 13}.get(size, size)
        other_state, other_first, other_last = exchange(state, first, last, flip)
        is_right = index // size % 2 == 1
        left_last = jnp.where(is_right, other_last, last)
        right_first = jnp.where(is_right, first, other_first)
        left_state = jnp.where(is_right, other_state, state)
        right_state = jnp.where(is_right, state, other_state)
        joined = jnp.concatenate([left_last[1:], right_first], axis=1)
        edge = sum(taps[1:, i, None, :] * joined[:, PAD - i : 2 * PAD - i, :] for i in range(tap_count))
        gates = rounded(edge[0] * edge[1])
        edge_state = jnp.zeros_like(state)
        for t in range(halo_rows):
            edge_state = decayed(1.0) * edge_state + gates[t][None, :]
        offset = (index % size * tokens).astype(jnp.float32)
        is_first = index % size == 0
        arriving = decayed(offset) * left_state
        arriving = arriving + jnp.where(is_first, 0.0, decayed(jnp.maximum(offset - halo_rows, 0.0))) * edge_state
        prefix = jnp.where(is_right, prefix + arriving, prefix)
        halo = jnp.where(is_right & is_first, other_last, halo)
        block = float(size * tokens)
        state = right_state + decayed(block - halo_rows) * edge_state + decayed(block) * left_state
        first = jnp.where(is_right, other_first, first)
        last = jnp.where(is_right, last, other_last)
        size *= 2
        if size * 2 == count:
            state, local, gate = lax.optimization_barrier((state, local, gate))
    return pl.pallas_call(
        final_kernel,
        out_shape=jax.ShapeDtypeStruct((tokens, channels), jnp.bfloat16),
        grid=grid,
        in_specs=[
            modes_spec, modes_spec, taps_spec, by_lanes(1), modes_spec, by_lanes(3, PAD), by_lanes(3, PAD),
            ends_spec, grid_spec, grid_spec, grid_spec,
        ],
        out_specs=by_lanes(tokens),
        scratch_shapes=[
            pltpu.VMEM((3, 2 * PAD, LANES), jnp.float32),
            pltpu.VMEM((tokens, LANES), jnp.float32),
        ],
        compiler_params=PARAMS,
        name="final",
    )(rates_own, scale, taps, skip_row, prefix, halo, head, ends, gated, local, gate)


def solution(mesh):
    in_specs = (P(None, "seq", "fft"), P(None, None, "fft"), P(), P(), P("fft"))
    out_specs = P("seq", "fft")
    return jax.shard_map(on_device, mesh=mesh, in_specs=in_specs, out_specs=out_specs, check_vma=False)
```

time: 107 us -> 25.1 us (0.23)
  other arithmetic: 27.2 us -> 0.54 us
  matrix products: 25.1 us -> 0 us
  blocking collectives: 14.6 us -> 0 us
  local copies, waits for them, and re-layouts: 14.7 us -> 1.51 us
  Pallas kernels: 0 us -> 6.1 us
  starting transfers between devices: 12.6 us -> 8.81 us
  waiting for transfers between devices: 11.1 us -> 7.59 us
    dot_general x16 -> x0, matrix products: 25.1 us -> none  [the longest x4 7.35 us: mix_along(): jnp.einsum(pattern, matrix[1], values[1], precision=highest)]
    all_to_all x1 -> x0, blocking collectives: 14.6 us -> none  [long_convolution(): lax.all_to_all(result.astype(jnp.bfloat16), 'seq', split_axis=1, concat_a...]
    sub x17 -> x0, other arithmetic: 12.7 us -> none  [the longest x16 12.5 us: add_mode(): spec_imag - weight_now * denom_imag]
    all_to_all x1 -> x0, waiting for transfers between devices: 11.1 us -> none  [long_convolution(): lax.all_to_all(gated_input.T, 'seq', split_axis=0, concat_axis=1, tiled=T...]
    mul x51 -> x0, other arithmetic: 8.32 us -> none  [the longest x16 7.03 us: add_mode(): denom_imag = decay_now * full_sine]
    all_to_all x1 -> x0, starting transfers between devices: 7.69 us -> none  [long_convolution(): lax.all_to_all(gated_input.T, 'seq', split_axis=0, concat_axis=1, tiled=T...]
    ppermute x1 -> x4, waiting for transfers between devices: 0.01 us -> 7.59 us  [exchange(): lax.ppermute(packed, 'seq', [(i, i ^ flip) for i in range(count)])]
    pallas_call x0 -> x3, Pallas kernels: none -> 6.1 us  [the longest x1 2.56 us: on_device(): pl.pallas_call(state_kernel, out_shape=(shape32(length, CHUNKS, channels)...]
  transfers between devices with their start and end apart: 2 -> 4, of which waited for: 1 -> 4; matrix products, arithmetic and copies ran while one was open for 30% -> 0% of each run, Pallas kernels for 0% -> 7%
where the time goes in v1:
time: 25.1 us; the launch traced here: 24.9 us
  starting transfers between devices  8.81 us (35%)
  waiting for transfers between devices  7.59 us (30%)
  Pallas kernels  6.1 us (24%)
  local copies, waits for them, and re-layouts  1.51 us (6%)
  other arithmetic  0.54 us (2%)
  between operations  0.37 us (1%)
    ppermute x4, starting transfers between devices, exchange(): lax.ppermute(packed, 'seq', [(i, i ^ flip) for i in range(count)])  8.81 us
    ppermute x4, waiting for transfers between devices, exchange(): lax.ppermute(packed, 'seq', [(i, i ^ flip) for i in range(count)])  7.59 us
    pallas_call x1, Pallas kernels, on_device(): pl.pallas_call(state_kernel, out_shape=(shape32(length, CHUNKS, channels)...  2.56 us
    pallas_call x1, Pallas kernels, on_device(): pl.pallas_call(final_kernel, out_shape=jax.ShapeDtypeStruct((tokens, chan...  1.82 us
    pallas_call x1, Pallas kernels, on_device(): pl.pallas_call(local_kernel, out_shape=(shape32(length, CHUNKS, channels)...  1.72 us
    unnamed x12, local copies, waits for them, and re-layouts  1.44 us
  transfers between devices with their start and end apart: 4, of which 4 were waited for; matrix products, arithmetic and copies ran while one was open for 0% of the time, Pallas kernels for 7%

profile of v1, /device:TPU:1, one launch (start us, length us, event | category | flops | bytes accessed | tf_op | source)
XLA Modules:
  0.0 24.9 jit_solution(6153473712798983269)
XLA Ops:
  0.0 0.0 copy-start.1
  0.0 0.7 %copy-done.1 = f32[7,3,256]{2,0,1:T(8,128)S(1)} copy-done((f32[7,3,256]{2,0,1:T(8,128)S(1)}, f32[7,3,256]{2,0,1:T(8,128)}, u32[]{:S(2)}) %copy-start.1) | copy-done | bytes 21528
  0.7 2.6 %state.1 = (f32[64,8,256]{2,1,0:T(8,128)S(1)}, f32[16,8,256]{2,1,0:T(8,128)S(1)}, f32[16,256]{1,0:T(8,128)S(1)}, f32[3,8,256]{2,1,0:T(8,128)S(1)}, f32[3,8,256]{...) custom-call(f32[16,4096]{1,0:T(8,128)} %bitcast.117, f32[16,4096]{1,0:T(8,128)} %bitcast.118, ...), custom_call_target="tpu_custom_call" | custom-call | tf_op jit(solution)/shard_map/state/pallas_call | solution.py:225
  3.4 3.3 %collective-permute-start = (bf16[72,256]{1,0:T(8,128)(2,1)S(1)}, bf16[72,256]{1,0:T(8,128)(2,1)S(1)}, u32[]{:S(2)}, u32[]{:S(2)}) collective-permute-start(bf16[72,256]{1,0:T(8,128)(2,1)S(1)} %pad_maximum_fusion), channel_id=1, source_target_pairs={{0,16},{16,0},{32,48},{48,32},{64,80},{80,64},{96,112},{112,96},{1... | collective-permute-start | bytes 110600 | tf_op jit(solution)/shard_map/ppermute | solution.py:273
  6.7 0.0 copy-start
  6.8 0.8 %collective-permute-done = bf16[72,256]{1,0:T(8,128)(2,1)S(1)} collective-permute-done((bf16[72,256]{1,0:T(8,128)(2,1)S(1)}, bf16[72,256]{1,0:T(8,128)(2,1)S(1)}, u32[]{:S(2)}, u32[]{:S(2)}) %collective-permute-start) | collective-permute-done | bytes 36896 | tf_op jit(solution)/shard_map/ppermute | solution.py:273
  7.7 0.2 collective-permute-start.1
  8.0 3.3 %collective-permute-done.1 = bf16[72,256]{1,0:T(8,128)(2,1)S(1)} collective-permute-done((bf16[72,256]{1,0:T(8,128)(2,1)S(1)}, bf16[72,256]{1,0:T(8,128)(2,1)S(1)}, u32[]{:S(2)}, u32[]{:S(2)}) %collective-permute-start.1) | collective-permute-done | bytes 36896 | tf_op jit(solution)/shard_map/ppermute | solution.py:273
  11.5 0.0 copy-start.2
  11.5 1.5 %collective-permute-start.2 = (bf16[72,256]{1,0:T(8,128)(2,1)S(1)}, bf16[72,256]{1,0:T(8,128)(2,1)S(1)}, u32[]{:S(2)}, u32[]{:S(2)}) collective-permute-start(bf16[72,256]{1,0:T(8,128)(2,1)S(1)} %pad_maximum_fusion.2), channel_id=1, source_target_pairs={{0,80},{16,64},{32,112},{48,96},{64,16},{80,0},{96,48},{112,32},{1... | collective-permute-start | bytes 110600 | tf_op jit(solution)/shard_map/ppermute | solution.py:273
  13.0 0.0 copy-start.3
  13.0 0.0 copy-done
  13.0 0.0 copy-done.2
  13.0 0.7 %copy-done.3 = f32[256]{0:T(256)S(1)} copy-done((f32[256]{0:T(256)S(1)}, f32[256]{0:T(256)}, u32[]{:S(2)}) %copy-start.3) | copy-done | bytes 1048
  13.7 1.7 %local.1 = (f32[64,8,256]{2,1,0:T(8,128)S(1)}, f32[64,8,256]{2,1,0:T(8,128)S(1)}, f32[1,256]{1,0:T(1,128)S(1)}) custom-call(f32[16,256]{1,0:T(8,128)S(1)} %get-tuple-element.18.rates_ref, f32[16,256]{1,0:T(8,128)S(1)} %get-tuple-element.19.scale_ref, f32[3,7,256]{2,1,0:T(8,128)S(1)} %bitcast.114, f32[1,256]{1,0:T(1,128)S(1)} %bitcast.116, ...), custom_call_target="tpu_custom_call" | custom-call | tf_op jit(solution)/shard_map/local/pallas_call | solution.py:255
  15.4 1.5 %collective-permute-done.2 = bf16[72,256]{1,0:T(8,128)(2,1)S(1)} collective-permute-done((bf16[72,256]{1,0:T(8,128)(2,1)S(1)}, bf16[72,256]{1,0:T(8,128)(2,1)S(1)}, u32[]{:S(2)}, u32[]{:S(2)}) %collective-permute-start.2) | collective-permute-done | bytes 36896 | tf_op jit(solution)/shard_map/ppermute | solution.py:273
  17.1 3.7 %collective-permute-start.3 = (bf16[72,256]{1,0:T(8,128)(2,1)S(1)}, bf16[72,256]{1,0:T(8,128)(2,1)S(1)}, u32[]{:S(2)}, u32[]{:S(2)}) collective-permute-start(bf16[72,256]{1,0:T(8,128)(2,1)S(1)} %pad_maximum_fusion.3), channel_id=1, source_target_pairs={{0,208},{16,192},{32,240},{48,224},{64,144},{80,128},{96,176},{112... | collective-permute-start | bytes 110600 | tf_op jit(solution)/shard_map/ppermute | solution.py:273
  20.8 2.0 %collective-permute-done.3 = bf16[72,256]{1,0:T(8,128)(2,1)S(1)} collective-permute-done((bf16[72,256]{1,0:T(8,128)(2,1)S(1)}, bf16[72,256]{1,0:T(8,128)(2,1)S(1)}, u32[]{:S(2)}, u32[]{:S(2)}) %collective-permute-start.3) | collective-permute-done | bytes 36896 | tf_op jit(solution)/shard_map/ppermute | solution.py:273
  23.0 0.1 add_select_fusion.incoming_ref
  23.1 1.8 %final.1 = bf16[512,256]{1,0:T(8,128)(2,1)} custom-call(f32[16,256]{1,0:T(8,128)S(1)} %get-tuple-element.18.rates_ref, f32[16,256]{1,0:T(8,128)S(1)} %get-tuple-element.19.scale_ref, f32[3,7,256]{2,1,0:T(8,128)S(1)} %bitcast.115, f32[1,256]{1,0:T(1,128)S(1)} %get-tuple-element.21.skip_ref, f32[16,256]{1,0:T(8,128)S(1)} %add_select_fusion.incoming_ref, ...), custom_call_target="tpu_custom_call" | custom-call | tf_op jit(solution)/shard_map/final/pallas_call | solution.py:308
  (50 shorter events, 0.5 us)
Async XLA Ops:
  0.0 0.7 %copy-start.1 = (f32[7,3,256]{2,0,1:T(8,128)S(1)}, f32[7,3,256]{2,0,1:T(8,128)}, u32[]{:S(2)}) copy-start(f32[7,3,256]{2,0,1:T(8,128)} %param.6) | copy-start | bytes 64516
  3.4 4.2 %collective-permute-start = (bf16[72,256]{1,0:T(8,128)(2,1)S(1)}, bf16[72,256]{1,0:T(8,128)(2,1)S(1)}, u32[]{:S(2)}, u32[]{:S(2)}) collective-permute-start(bf16[72,256]{1,0:T(8,128)(2,1)S(1)} %pad_maximum_fusion), channel_id=1, source_target_pairs={{0,16},{16,0},{32,48},{48,32},{64,80},{80,64},{96,112},{112,96},{1... | collective-permute-start | bytes 110600 | tf_op jit(solution)/shard_map/ppermute | solution.py:273
  6.7 6.3 %copy-start = (bf16[3,512,256]{2,1,0:T(8,128)(2,1)S(1)}, bf16[3,512,256]{2,1,0:T(8,128)(2,1)}, u32[]{:S(2)}) copy-start(bf16[3,512,256]{2,1,0:T(8,128)(2,1)} %zeroth_ref.1) | copy-start | bytes 2359300
  7.7 3.5 %collective-permute-start.1 = (bf16[72,256]{1,0:T(8,128)(2,1)S(1)}, bf16[72,256]{1,0:T(8,128)(2,1)S(1)}, u32[]{:S(2)}, u32[]{:S(2)}) collective-permute-start(bf16[72,256]{1,0:T(8,128)(2,1)S(1)} %pad_maximum_fusion.1), channel_id=1, source_target_pairs={{0,48},{16,32},{32,16},{48,0},{64,112},{80,96},{96,80},{112,64},{1... | collective-permute-start | bytes 110600 | tf_op jit(solution)/shard_map/ppermute | solution.py:273
  11.5 1.5 %copy-start.2 = (f32[7,3,256]{2,0,1:T(8,128)S(1)}, f32[7,3,256]{2,0,1:T(8,128)}, u32[]{:S(2)}) copy-start(f32[7,3,256]{2,0,1:T(8,128)} %param.6) | copy-start | bytes 64516
  11.5 5.4 %collective-permute-start.2 = (bf16[72,256]{1,0:T(8,128)(2,1)S(1)}, bf16[72,256]{1,0:T(8,128)(2,1)S(1)}, u32[]{:S(2)}, u32[]{:S(2)}) collective-permute-start(bf16[72,256]{1,0:T(8,128)(2,1)S(1)} %pad_maximum_fusion.2), channel_id=1, source_target_pairs={{0,80},{16,64},{32,112},{48,96},{64,16},{80,0},{96,48},{112,32},{1... | collective-permute-start | bytes 110600 | tf_op jit(solution)/shard_map/ppermute | solution.py:273
  13.0 0.7 %copy-start.3 = (f32[256]{0:T(256)S(1)}, f32[256]{0:T(256)}, u32[]{:S(2)}) copy-start(f32[256]{0:T(256)} %param.9) | copy-start | bytes 3076
  17.1 5.8 %collective-permute-start.3 = (bf16[72,256]{1,0:T(8,128)(2,1)S(1)}, bf16[72,256]{1,0:T(8,128)(2,1)S(1)}, u32[]{:S(2)}, u32[]{:S(2)}) collective-permute-start(bf16[72,256]{1,0:T(8,128)(2,1)S(1)} %pad_maximum_fusion.3), channel_id=1, source_target_pairs={{0,208},{16,192},{32,240},{48,224},{64,144},{80,128},{96,176},{112... | collective-permute-start | bytes 110600 | tf_op jit(solution)/shard_map/ppermute | solution.py:273

commit v2 on v1

--- a/solution.py
+++ b/solution.py
@@ -47,7 +47,8 @@
 
 
 def state_kernel(
-    rates_hbm, residues_hbm, taps_ref, tokens_hbm, gated_ref, ends_ref, state_ref, head_ref, tail_ref, rates_ref, scale_ref,
+    rates_hbm, residues_hbm, taps_hbm, skip_hbm, tokens_hbm,
+    gated_ref, ends_ref, state_ref, head_ref, tail_ref, rates_ref, scale_ref, taps_ref, skip_ref,
     bits_ref, head_bits_ref, tail_bits_ref, residues_ref, one_ref, two_ref, sems,
 ):
     channels = rates_ref.shape[1]
@@ -67,6 +68,10 @@
             )
             copy.start()
             loads.append(copy)
+    early = [
+        pltpu.make_async_copy(taps_hbm, taps_ref, sems.at[2 * halves + 4]),
+        pltpu.make_async_copy(skip_hbm, skip_ref, sems.at[2 * halves + 5]),
+    ]
     late = [
         pltpu.make_async_copy(rates_hbm.at[:, pl.ds(start, channels)], rates_ref, sems.at[2 * halves]),
         pltpu.make_async_copy(residues_hbm.at[:, pl.ds(start, channels)], residues_ref, sems.at[2 * halves + 1]),
@@ -75,12 +80,14 @@
             tokens_hbm.at[0, token_count - edge_rows : token_count, :], tail_bits_ref, sems.at[2 * halves + 3]
         ),
     ]
-    for copy in late:
+    for copy in early + late:
         copy.start()
     sublane = lax.broadcasted_iota(jnp.int32, (CHUNKS, LANES), 0)
     keep = jnp.where(sublane == 0, jnp.where(lax.axis_index("seq") == 0, 1.0, 0.0), 1.0)
     to_end = -((CHUNKS - 1 - sublane) * length).astype(jnp.float32)
     zero_rows = jnp.zeros((PAD, LANES), jnp.float32)
+    for copy in early:
+        copy.wait()
     for half in range(halves):
         lanes = slice(half * LANES, (half + 1) * LANES)
         for buffer, q in ((one_ref, 1), (two_ref, 2)):
@@ -121,12 +128,11 @@
 
 
 def local_kernel(
-    rates_ref, scale_ref, taps_ref, skip_ref, zeroth_ref, gated_ref, local_ref, gate_ref, skip_row_ref, buffer_ref
+    rates_ref, scale_ref, taps_ref, zeroth_ref, gated_ref, local_ref, gate_ref, buffer_ref
 ):
     length = zeroth_ref.shape[1] // CHUNKS
     mode_count = rates_ref.shape[0]
     tap_count = taps_ref.shape[1]
-    skip_row_ref[...] = skip_ref[...]
     buffer_ref[0:PAD, :] = jnp.zeros((PAD, LANES), jnp.float32)
     buffer_ref[PAD:, :] = zeroth_ref[0].astype(jnp.float32)
 
@@ -222,7 +228,7 @@
     taps = taps.transpose(1, 0, 2)
     hbm = pl.BlockSpec(memory_space=pltpu.HBM)
     vmem = pl.BlockSpec(memory_space=pltpu.VMEM)
-    gated, ends, state, head, tail, rates_own, scale = pl.pallas_call(
+    gated, ends, state, head, tail, rates_own, scale, taps, skip = pl.pallas_call(
         state_kernel,
         out_shape=(
             shape32(length, CHUNKS, channels),
@@ -232,9 +238,11 @@
             shape32(3, PAD, channels),
             shape32(mode_count, channels),
             shape32(mode_count, channels),
+            shape32(3, tap_count, channels),
+            shape32(1, channels),
         ),
-        in_specs=[hbm, hbm, vmem, hbm],
-        out_specs=(vmem,) * 7,
+        in_specs=[hbm] * 5,
+        out_specs=(vmem,) * 9,
         scratch_shapes=[
             pltpu.VMEM((halves, 2, tokens, LANES), jnp.bfloat16),
             pltpu.VMEM((2 * PAD, channels), jnp.bfloat16),
@@ -242,69 +250,96 @@
             pltpu.VMEM((mode_count, channels), jnp.float32),
             pltpu.VMEM((halves, PAD + tokens, LANES), jnp.float32),
             pltpu.VMEM((halves, PAD + tokens, LANES), jnp.float32),
-            pltpu.SemaphoreType.DMA((2 * halves + 4,)),
+            pltpu.SemaphoreType.DMA((2 * halves + 6,)),
         ],
         compiler_params=PARAMS,
         name="state",
-    )(*(pltpu.with_memory_space_constraint(array, pltpu.HBM) for array in (rates.T, residues.T)), taps,
-      pltpu.with_memory_space_constraint(projections, pltpu.HBM))
+    )(*(
+        pltpu.with_memory_space_constraint(array, pltpu.HBM)
+        for array in (rates.T, residues.T, taps, skip[None, :], projections)
+    ))
     taps_spec = by_lanes(3, tap_count)
     modes_spec = by_lanes(mode_count)
     grid_spec = by_lanes(length, CHUNKS)
     ends_spec = by_lanes(mode_count, CHUNKS)
-    local, gate, skip_row = pl.pallas_call(
+    local, gate = pl.pallas_call(
         local_kernel,
-        out_shape=(shape32(length, CHUNKS, channels),) * 2 + (shape32(1, channels),),
+        out_shape=(shape32(length, CHUNKS, channels),) * 2,
         grid=grid,
-        in_specs=[modes_spec, modes_spec, taps_spec, by_lanes(1), one_projection(0, tokens), grid_spec],
-        out_specs=(grid_spec, grid_spec, by_lanes(1)),
+        in_specs=[modes_spec, modes_spec, taps_spec, one_projection(0, tokens), grid_spec],
+        out_specs=(grid_spec, grid_spec),
         scratch_shapes=[pltpu.VMEM((PAD + tokens, LANES), jnp.float32)],
         compiler_params=PARAMS,
         name="local",
-    )(rates_own, scale, taps, skip[None, :], projections, gated)
+    )(rates_own, scale, taps, projections, gated)
 
     def decayed(steps):
         return jnp.exp(-rates_own * jnp.asarray(steps, jnp.float32))
 
-    def exchange(state, first, last, flip):
+    def pack(state, first, last):
         high = lax.reduce_precision(state, 8, 7)
         rows = [high, state - high, last.reshape(3 * PAD, channels), first.reshape(2 * PAD, channels)]
-        packed = jnp.concatenate(rows, axis=0).astype(jnp.bfloat16)
-        packed = lax.ppermute(packed, "seq", [(i, i ^ flip) for i in range(count)]).astype(jnp.float32)
+        return jnp.concatenate(rows, axis=0).astype(jnp.bfloat16)
+
+    def unpack(packed):
+        packed = packed.astype(jnp.float32)
         edges = packed[2 * mode_count :].reshape(5, PAD, channels)
         return packed[:mode_count] + packed[mode_count : 2 * mode_count], edges[3:], edges[:3]
 
-    halo = jnp.zeros_like(tail)
-    prefix = jnp.zeros_like(state)
-    first, last = head[1:], tail
-    size = 1
-    while size < count:
-        flip = {1: 1, 2: 3, 4: 5, 8: 13}.get(size, size)
-        other_state, other_first, other_last = exchange(state, first, last, flip)
-        is_right = index // size % 2 == 1
-        left_last = jnp.where(is_right, other_last, last)
-        right_first = jnp.where(is_right, first, other_first)
-        left_state = jnp.where(is_right, other_state, state)
-        right_state = jnp.where(is_right, state, other_state)
+    def send(packed, flip, devices):
+        return lax.ppermute(packed, "seq", [(i, i ^ flip) for i in devices])
+
+    def edge_state_of(left_last, right_first):
         joined = jnp.concatenate([left_last[1:], right_first], axis=1)
         edge = sum(taps[1:, i, None, :] * joined[:, PAD - i : 2 * PAD - i, :] for i in range(tap_count))
         gates = rounded(edge[0] * edge[1])
         edge_state = jnp.zeros_like(state)
         for t in range(halo_rows):
             edge_state = decayed(1.0) * edge_state + gates[t][None, :]
+        return edge_state
+
+    def arriving(left_state, edge_state, size):
         offset = (index % size * tokens).astype(jnp.float32)
-        is_first = index % size == 0
-        arriving = decayed(offset) * left_state
-        arriving = arriving + jnp.where(is_first, 0.0, decayed(jnp.maximum(offset - halo_rows, 0.0))) * edge_state
-        prefix = jnp.where(is_right, prefix + arriving, prefix)
-        halo = jnp.where(is_right & is_first, other_last, halo)
-        block = float(size * tokens)
-        state = right_state + decayed(block - halo_rows) * edge_state + decayed(block) * left_state
+        edge_part = decayed(jnp.maximum(offset - halo_rows, 0.0)) * edge_state
+        return decayed(offset) * left_state + jnp.where(index % size == 0, 0.0, edge_part)
+
+    def join(block, received, prefix, halo, size):
+        state, first, last = block
+        other_state, other_first, other_last = unpack(received)
+        is_right = index // size % 2 == 1
+        left_last = jnp.where(is_right, other_last, last)
+        right_first = jnp.where(is_right, first, other_first)
+        left_state = jnp.where(is_right, other_state, state)
+        right_state = jnp.where(is_right, state, other_state)
+        edge_state = edge_state_of(left_last, right_first)
+        prefix = jnp.where(is_right, prefix + arriving(left_state, edge_state, size), prefix)
+        halo = jnp.where(is_right & (index % size == 0), other_last, halo)
+        steps = float(size * tokens)
+        state = right_state + decayed(steps - halo_rows) * edge_state + decayed(steps) * left_state
         first = jnp.where(is_right, other_first, first)
         last = jnp.where(is_right, last, other_last)
-        size *= 2
-        if size * 2 == count:
-            state, local, gate = lax.optimization_barrier((state, local, gate))
+        return (state, first, last), prefix, halo
+
+    everyone, early, late = range(count), range(count // 2), range(count // 2, count)
+    block, prefix, halo = (state, head[1:], tail), jnp.zeros_like(state), jnp.zeros_like(tail)
+    block, prefix, halo = join(block, send(pack(*block), 1, everyone), prefix, halo, 1)
+    received = send(pack(*block), 3, everyone)
+    received, local, gate = lax.optimization_barrier((received, local, gate))
+    block, prefix, halo = join(block, received, prefix, halo, 2)
+    packed = pack(*block)
+    received = send(packed, 5, early)
+    joined, _, _ = join(block, received, prefix, halo, 4)
+    total = pack(*joined)
+    crossed = send(total, 13, early)
+    left_state, _, left_last = unpack(crossed)
+    offset = (index % (count // 2) * tokens).astype(jnp.float32)
+    is_late = index >= count // 2
+    prefix = prefix + jnp.where(is_late, decayed(offset), 0.0) * left_state
+    second, prefix, left_last = lax.optimization_barrier((send(packed, 5, late), prefix, left_last))
+    (_, first, _), prefix, halo = join(block, received + second, prefix, halo, 4)
+    edge_part = decayed(jnp.maximum(offset - halo_rows, 0.0)) * edge_state_of(left_last, first)
+    prefix = prefix + jnp.where(index > count // 2, edge_part, 0.0)
+    halo = jnp.where(index == count // 2, left_last, halo)
     return pl.pallas_call(
         final_kernel,
         out_shape=jax.ShapeDtypeStruct((tokens, channels), jnp.bfloat16),
@@ -320,7 +355,7 @@
         ],
         compiler_params=PARAMS,
         name="final",
-    )(rates_own, scale, taps, skip_row, prefix, halo, head, ends, gated, local, gate)
+    )(rates_own, scale, taps, skip, prefix, halo, head, ends, gated, local, gate)
 
 
 def solution(mesh):

time: 25.1 us -> 22.9 us (0.912)
  local copies, waits for them, and re-layouts: 1.51 us -> 0.1 us
  waiting for transfers between devices: 7.59 us -> 6.51 us
    unnamed x12 -> x6, local copies, waits for them, and re-layouts: 1.44 us -> 0.02 us
    ppermute x4 -> x5, waiting for transfers between devices: 7.59 us -> 6.51 us  [send(): return lax.ppermute(packed, 'seq', [(i, i ^ flip) for i in devices])]
    ppermute x4 -> x5, starting transfers between devices: 8.81 us -> 8.9 us  [send(): return lax.ppermute(packed, 'seq', [(i, i ^ flip) for i in devices])]
  transfers between devices with their start and end apart: 4 -> 5, of which waited for: 4 -> 4; matrix products, arithmetic and copies ran while one was open for 0% -> 0% of each run, Pallas kernels for 7% -> 8%
where the time goes in v2:
time: 22.9 us; the launch traced here: 22.8 us
  starting transfers between devices  8.9 us (39%)
  waiting for transfers between devices  6.51 us (28%)
  Pallas kernels  6.16 us (27%)
  other arithmetic  0.55 us (2%)
  between operations  0.54 us (2%)
    ppermute x5, starting transfers between devices, send(): return lax.ppermute(packed, 'seq', [(i, i ^ flip) for i in devices])  8.9 us
    ppermute x5, waiting for transfers between devices, send(): return lax.ppermute(packed, 'seq', [(i, i ^ flip) for i in devices])  6.51 us
    pallas_call x1, Pallas kernels, on_device(): pl.pallas_call(state_kernel, out_shape=(shape32(length, CHUNKS, channels)...  2.62 us
    pallas_call x1, Pallas kernels, on_device(): pl.pallas_call(final_kernel, out_shape=jax.ShapeDtypeStruct((tokens, chan...  1.82 us
    pallas_call x1, Pallas kernels, on_device(): pl.pallas_call(local_kernel, out_shape=(shape32(length, CHUNKS, channels)...  1.72 us
  transfers between devices with their start and end apart: 5, of which 4 were waited for; matrix products, arithmetic and copies ran while one was open for 0% of the time, Pallas kernels for 8%

profile of v2, /device:TPU:1, one launch (start us, length us, event | category | flops | bytes accessed | tf_op | source)
XLA Modules:
  0.0 22.8 jit_solution(5136268676865556629)
XLA Ops:
  0.0 2.6 %state.1 = (f32[64,8,256]{2,1,0:T(8,128)S(1)}, f32[16,8,256]{2,1,0:T(8,128)S(1)}, f32[16,256]{1,0:T(8,128)S(1)}, f32[3,8,256]{2,1,0:T(8,128)S(1)}, f32[3,8,256]{...) custom-call(f32[16,4096]{1,0:T(8,128)} %bitcast.117, ...), custom_call_target="tpu_custom_call" | custom-call | tf_op jit(solution)/shard_map/state/pallas_call | solution.py:231
  2.6 0.0 copy-start
  2.7 3.3 %collective-permute-start = (bf16[72,256]{1,0:T(8,128)(2,1)S(1)}, bf16[72,256]{1,0:T(8,128)(2,1)S(1)}, u32[]{:S(2)}, u32[]{:S(2)}) collective-permute-start(bf16[72,256]{1,0:T(8,128)(2,1)S(1)} %pad_maximum_fusion), channel_id=1, source_target_pairs={{0,16},{16,0},{32,48},{48,32},{64,80},{80,64},{96,112},{112,96},{1... | collective-permute-start | bytes 110600 | tf_op jit(solution)/shard_map/ppermute | solution.py:290
  6.1 0.8 %collective-permute-done = bf16[72,256]{1,0:T(8,128)(2,1)S(1)} collective-permute-done((bf16[72,256]{1,0:T(8,128)(2,1)S(1)}, bf16[72,256]{1,0:T(8,128)(2,1)S(1)}, u32[]{:S(2)}, u32[]{:S(2)}) %collective-permute-start) | collective-permute-done | bytes 36896 | tf_op jit(solution)/shard_map/ppermute | solution.py:290
  7.1 0.2 collective-permute-start.1
  7.3 0.0 copy-done
  7.3 1.7 %local.1 = (f32[64,8,256]{2,1,0:T(8,128)S(1)}, f32[64,8,256]{2,1,0:T(8,128)S(1)}) custom-call(f32[16,256]{1,0:T(8,128)S(1)} %get-tuple-element.22.rates_ref, f32[16,256]{1,0:T(8,128)S(1)} %get-tuple-element.23.scale_ref, f32[3,7,256]{2,1,0:T(8,128)S(1)} %get-tuple-element.24.taps_ref, bf16[3,512,256]{2,1,0:T(8,128)(2,1)S(1)} %copy-done, ...), custom_call_target="tpu_custom_call" | custom-call | tf_op jit(solution)/shard_map/local/pallas_call | solution.py:265
  9.0 1.6 %collective-permute-done.1 = bf16[72,256]{1,0:T(8,128)(2,1)S(1)} collective-permute-done((bf16[72,256]{1,0:T(8,128)(2,1)S(1)}, bf16[72,256]{1,0:T(8,128)(2,1)S(1)}, u32[]{:S(2)}, u32[]{:S(2)}) %collective-permute-start.1) | collective-permute-done | bytes 36896 | tf_op jit(solution)/shard_map/ppermute | solution.py:290
  10.8 3.4 %collective-permute-start.3 = (bf16[72,256]{1,0:T(8,128)(2,1)S(1)}, bf16[72,256]{1,0:T(8,128)(2,1)S(1)}, u32[]{:S(2)}, u32[]{:S(2)}) collective-permute-start(bf16[72,256]{1,0:T(8,128)(2,1)S(1)} %pad_maximum_fusion.2), channel_id=1, source_target_pairs={{0,80},{16,64},{32,112},{48,96},{64,16},{80,0},{96,48},{112,32},{1... | collective-permute-start | bytes 110600 | tf_op jit(solution)/shard_map/ppermute | solution.py:290
  14.2 3.8 %collective-permute-done.3 = bf16[72,256]{1,0:T(8,128)(2,1)S(1)} collective-permute-done((bf16[72,256]{1,0:T(8,128)(2,1)S(1)}, bf16[72,256]{1,0:T(8,128)(2,1)S(1)}, u32[]{:S(2)}, u32[]{:S(2)}) %collective-permute-start.3) | collective-permute-done | bytes 36896 | tf_op jit(solution)/shard_map/ppermute | solution.py:290
  18.2 1.3 %collective-permute-start.4 = (bf16[72,256]{1,0:T(8,128)(2,1)S(1)}, bf16[72,256]{1,0:T(8,128)(2,1)S(1)}, u32[]{:S(2)}, u32[]{:S(2)}) collective-permute-start(bf16[72,256]{1,0:T(8,128)(2,1)S(1)} %pad_maximum_fusion.3), channel_id=1, source_target_pairs={{0,208},{16,192},{32,240},{48,224},{64,144},{80,128},{96,176},{112... | collective-permute-start | bytes 110600 | tf_op jit(solution)/shard_map/ppermute | solution.py:290
  19.6 0.7 %collective-permute-start.2 = (bf16[72,256]{1,0:T(8,128)(2,1)S(1)}, bf16[72,256]{1,0:T(8,128)(2,1)S(1)}, u32[]{:S(2)}, u32[]{:S(2)}) collective-permute-start(bf16[72,256]{1,0:T(8,128)(2,1)S(1)} %pad_maximum_fusion.2), channel_id=1, source_target_pairs={{128,208},{144,192},{160,240},{176,224},{192,144},{208,128},{224,1... | collective-permute-start | bytes 110600 | tf_op jit(solution)/shard_map/ppermute | solution.py:290
  20.2 0.4 %collective-permute-done.4 = bf16[72,256]{1,0:T(8,128)(2,1)S(1)} collective-permute-done((bf16[72,256]{1,0:T(8,128)(2,1)S(1)}, bf16[72,256]{1,0:T(8,128)(2,1)S(1)}, u32[]{:S(2)}, u32[]{:S(2)}) %collective-permute-start.4) | collective-permute-done | bytes 36896 | tf_op jit(solution)/shard_map/ppermute | solution.py:290
  20.7 0.0 collective-permute-done.2
  20.8 0.1 fusion.25
  20.9 1.8 %final.1 = bf16[512,256]{1,0:T(8,128)(2,1)} custom-call(f32[16,256]{1,0:T(8,128)S(1)} %get-tuple-element.22.rates_ref, f32[16,256]{1,0:T(8,128)S(1)} %get-tuple-element.23.scale_ref, f32[3,7,256]{2,1,0:T(8,128)S(1)} %get-tuple-element.24.taps_ref, f32[1,256]{1,0:T(1,128)S(1)} %get-tuple-element.25.skip_ref, f32[16,256]{1,0:T(8,128)S(1)} %fusion.5.incoming_ref, ...), custom_call_target="tpu_custom_call" | custom-call | tf_op jit(solution)/shard_map/final/pallas_call | solution.py:343
  (56 shorter events, 0.6 us)
Async XLA Ops:
  2.6 4.7 %copy-start = (bf16[3,512,256]{2,1,0:T(8,128)(2,1)S(1)}, bf16[3,512,256]{2,1,0:T(8,128)(2,1)}, u32[]{:S(2)}) copy-start(bf16[3,512,256]{2,1,0:T(8,128)(2,1)} %zeroth_ref.1) | copy-start | bytes 2359300
  2.7 4.2 %collective-permute-start = (bf16[72,256]{1,0:T(8,128)(2,1)S(1)}, bf16[72,256]{1,0:T(8,128)(2,1)S(1)}, u32[]{:S(2)}, u32[]{:S(2)}) collective-permute-start(bf16[72,256]{1,0:T(8,128)(2,1)S(1)} %pad_maximum_fusion), channel_id=1, source_target_pairs={{0,16},{16,0},{32,48},{48,32},{64,80},{80,64},{96,112},{112,96},{1... | collective-permute-start | bytes 110600 | tf_op jit(solution)/shard_map/ppermute | solution.py:290
  7.1 3.5 %collective-permute-start.1 = (bf16[72,256]{1,0:T(8,128)(2,1)S(1)}, bf16[72,256]{1,0:T(8,128)(2,1)S(1)}, u32[]{:S(2)}, u32[]{:S(2)}) collective-permute-start(bf16[72,256]{1,0:T(8,128)(2,1)S(1)} %pad_maximum_fusion.1), channel_id=1, source_target_pairs={{0,48},{16,32},{32,16},{48,0},{64,112},{80,96},{96,80},{112,64},{1... | collective-permute-start | bytes 110600 | tf_op jit(solution)/shard_map/ppermute | solution.py:290
  10.8 7.2 %collective-permute-start.3 = (bf16[72,256]{1,0:T(8,128)(2,1)S(1)}, bf16[72,256]{1,0:T(8,128)(2,1)S(1)}, u32[]{:S(2)}, u32[]{:S(2)}) collective-permute-start(bf16[72,256]{1,0:T(8,128)(2,1)S(1)} %pad_maximum_fusion.2), channel_id=1, source_target_pairs={{0,80},{16,64},{32,112},{48,96},{64,16},{80,0},{96,48},{112,32},{1... | collective-permute-start | bytes 110600 | tf_op jit(solution)/shard_map/ppermute | solution.py:290
  18.2 2.4 %collective-permute-start.4 = (bf16[72,256]{1,0:T(8,128)(2,1)S(1)}, bf16[72,256]{1,0:T(8,128)(2,1)S(1)}, u32[]{:S(2)}, u32[]{:S(2)}) collective-permute-start(bf16[72,256]{1,0:T(8,128)(2,1)S(1)} %pad_maximum_fusion.3), channel_id=1, source_target_pairs={{0,208},{16,192},{32,240},{48,224},{64,144},{80,128},{96,176},{112... | collective-permute-start | bytes 110600 | tf_op jit(solution)/shard_map/ppermute | solution.py:290
  19.6 1.1 %collective-permute-start.2 = (bf16[72,256]{1,0:T(8,128)(2,1)S(1)}, bf16[72,256]{1,0:T(8,128)(2,1)S(1)}, u32[]{:S(2)}, u32[]{:S(2)}) collective-permute-start(bf16[72,256]{1,0:T(8,128)(2,1)S(1)} %pad_maximum_fusion.2), channel_id=1, source_target_pairs={{128,208},{144,192},{160,240},{176,224},{192,144},{208,128},{224,1... | collective-permute-start | bytes 110600 | tf_op jit(solution)/shard_map/ppermute | solution.py:290

commit v3 on v2

--- a/solution.py
+++ b/solution.py
@@ -127,85 +127,93 @@
             state_ref[m : m + 1, lanes] = jnp.sum(weight * states[m], axis=0, keepdims=True)
 
 
-def local_kernel(
-    rates_ref, scale_ref, taps_ref, zeroth_ref, gated_ref, local_ref, gate_ref, buffer_ref
-):
-    length = zeroth_ref.shape[1] // CHUNKS
+def local_kernel(rates_ref, scale_ref, taps_ref, tokens_ref, gated_ref, local_ref, gate_ref, buffer_ref):
+    length = gated_ref.shape[0]
     mode_count = rates_ref.shape[0]
     tap_count = taps_ref.shape[1]
-    buffer_ref[0:PAD, :] = jnp.zeros((PAD, LANES), jnp.float32)
-    buffer_ref[PAD:, :] = zeroth_ref[0].astype(jnp.float32)
-
-    def emit(j, row):
-        gate_ref[j] = row
-
-    filter_chunks(buffer_ref, [spread(taps_ref[0, i : i + 1, :]) for i in range(tap_count)], length, emit)
-    decay = jnp.exp(-rates_ref[...])
-    decays = [spread(decay[m : m + 1]) for m in range(mode_count)]
-    scales = [spread(scale_ref[m : m + 1, :]) for m in range(mode_count)]
-    states = [gated_ref[0]] * mode_count
-    for j in range(length):
-        if j > 0:
-            row = gated_ref[j]
-            states = [d * h + row for d, h in zip(decays, states)]
-        local_ref[j] = pairwise_sum([c * h for c, h in zip(scales, states)])
+    for half in range(rates_ref.shape[1] // LANES):
+        lanes = slice(half * LANES, (half + 1) * LANES)
+        buffer_ref[half, 0:PAD, :] = jnp.zeros((PAD, LANES), jnp.float32)
+        buffer_ref[half, PAD:, :] = tokens_ref[0, :, lanes].astype(jnp.float32)
+
+        def emit(j, row):
+            gate_ref[j, :, lanes] = row
+
+        rows = [spread(taps_ref[0, i : i + 1, lanes]) for i in range(tap_count)]
+        filter_chunks(buffer_ref.at[half], rows, length, emit)
+        decay = jnp.exp(-rates_ref[:, lanes])
+        decays = [spread(decay[m : m + 1]) for m in range(mode_count)]
+        scales = [spread(scale_ref[m : m + 1, lanes]) for m in range(mode_count)]
+        states = [gated_ref[0, :, lanes]] * mode_count
+        for j in range(length):
+            if j > 0:
+                row = gated_ref[j, :, lanes]
+                states = [d * h + row for d, h in zip(decays, states)]
+            local_ref[j, :, lanes] = pairwise_sum([c * h for c, h in zip(scales, states)])
+
+
+def late_kernel(*refs):
+    operands, rest = refs[:11], refs[12:]
+
+    @pl.when(lax.axis_index("seq") >= lax.axis_size("seq") // 2)
+    def _():
+        final_kernel(*operands, *rest)
 
 
 def final_kernel(
     rates_ref, scale_ref, taps_ref, skip_ref, incoming_ref, halo_ref, head_ref, ends_ref, gated_ref, local_ref,
-    gate_ref, out_ref, edge_ref, rows_ref,
+    gate_ref, out_hbm, edge_ref, rows_ref, out_ref, sems,
 ):
     length = gated_ref.shape[0]
     mode_count = rates_ref.shape[0]
     tap_count = taps_ref.shape[1]
     halo_rows = tap_count - 1
     sublane = lax.broadcasted_iota(jnp.int32, (CHUNKS, LANES), 0)
-    edges = []
-    for q in range(3):
-        edge_ref[q, 0:PAD, :] = halo_ref[q]
-        edge_ref[q, PAD : 2 * PAD, :] = head_ref[q, 0:PAD, :]
-        edges.append(
-            pairwise_sum([taps_ref[q, i : i + 1, :] * edge_ref[q, PAD - i : 2 * PAD - i, :] for i in range(tap_count)])
-        )
-    edge_gated = rounded(edges[1] * edges[2]) * jnp.where(lax.axis_index("seq") == 0, 0.0, 1.0)
-    rates = rates_ref[...]
-    scale = scale_ref[...]
-    decay = jnp.exp(-rates)
-    edge_state = jnp.zeros_like(decay)
-    for t in range(halo_rows):
-        edge_state = decay * edge_state + edge_gated[t : t + 1]
-    edge_state = edge_state * jnp.exp(-rates * float(length - halo_rows))
-    chunk_decay = jnp.exp(-rates * float(length))
-    decays = [spread(decay[m : m + 1]) for m in range(mode_count)]
-    states = []
-    for m in range(mode_count):
-        factor = spread(chunk_decay[m : m + 1])
-        ends = ends_ref[m] + jnp.where(sublane == 0, spread(edge_state[m : m + 1]), 0.0)
-        carried = jnp.where(sublane == 0, spread(incoming_ref[m : m + 1, :]), pltpu.roll(ends, 1, 0))
-        for distance in (1, 2, 4):
-            carried = carried + jnp.where(sublane >= distance, factor * pltpu.roll(carried, distance, 0), 0.0)
-            factor = factor * factor
-        states.append(carried * spread(scale[m : m + 1]))
-    skip = spread(skip_ref[...])
-    for j in range(length):
-        states = [d * h for d, h in zip(decays, states)]
-        gated, gate = gated_ref[j], gate_ref[j]
-        if j < halo_rows:
-            new = jnp.where(sublane == 0, spread(edge_gated[j : j + 1]), 0.0)
-            states = [h + spread(scale[m : m + 1]) * new for m, h in enumerate(states)]
-            gated = gated + new
-            gate = jnp.where(sublane == 0, spread(edges[0][j : j + 1]), gate)
-        long_out = rounded(local_ref[j] + pairwise_sum(states))
-        rows_ref[pl.ds(j, CHUNKS, stride=length), :] = gate * (long_out + skip * gated)
-    out_ref[...] = rows_ref[...].astype(jnp.bfloat16)
-
-
-def by_lanes(*dims):
-    return pl.BlockSpec((*dims, LANES), lambda i: (*(0 for _ in dims), i))
-
-
-def one_projection(q, tokens):
-    return pl.BlockSpec((1, tokens, LANES), lambda i: (q, 0, i))
+    is_new = jnp.where(lax.axis_index("seq") == 0, 0.0, 1.0)
+    copies = []
+    for half in range(rates_ref.shape[1] // LANES):
+        lanes = slice(half * LANES, (half + 1) * LANES)
+        edges = []
+        for q in range(3):
+            edge_ref[q, 0:PAD, :] = halo_ref[q, :, lanes]
+            edge_ref[q, PAD : 2 * PAD, :] = head_ref[q, :, lanes]
+            terms = [taps_ref[q, i : i + 1, lanes] * edge_ref[q, PAD - i : 2 * PAD - i, :] for i in range(tap_count)]
+            edges.append(pairwise_sum(terms))
+        edge_gated = rounded(edges[1] * edges[2]) * is_new
+        rates = rates_ref[:, lanes]
+        scale = scale_ref[:, lanes]
+        decay = jnp.exp(-rates)
+        edge_state = jnp.zeros_like(decay)
+        for t in range(halo_rows):
+            edge_state = decay * edge_state + edge_gated[t : t + 1]
+        edge_state = edge_state * jnp.exp(-rates * float(length - halo_rows))
+        chunk_decay = jnp.exp(-rates * float(length))
+        decays = [spread(decay[m : m + 1]) for m in range(mode_count)]
+        states = []
+        for m in range(mode_count):
+            factor = spread(chunk_decay[m : m + 1])
+            ends = ends_ref[m, :, lanes] + jnp.where(sublane == 0, spread(edge_state[m : m + 1]), 0.0)
+            carried = jnp.where(sublane == 0, spread(incoming_ref[m : m + 1, lanes]), pltpu.roll(ends, 1, 0))
+            for distance in (1, 2, 4):
+                carried = carried + jnp.where(sublane >= distance, factor * pltpu.roll(carried, distance, 0), 0.0)
+                factor = factor * factor
+            states.append(carried * spread(scale[m : m + 1]))
+        skip = spread(skip_ref[:, lanes])
+        for j in range(length):
+            states = [d * h for d, h in zip(decays, states)]
+            gated, gate = gated_ref[j, :, lanes], gate_ref[j, :, lanes]
+            if j < halo_rows:
+                new = jnp.where(sublane == 0, spread(edge_gated[j : j + 1]), 0.0)
+                states = [h + spread(scale[m : m + 1]) * new for m, h in enumerate(states)]
+                gated = gated + new
+                gate = jnp.where(sublane == 0, spread(edges[0][j : j + 1]), gate)
+            long_out = rounded(local_ref[j, :, lanes] + pairwise_sum(states))
+            rows_ref[half, pl.ds(j, CHUNKS, stride=length), :] = gate * (long_out + skip * gated)
+        out_ref[half] = rows_ref[half].astype(jnp.bfloat16)
+        copies.append(pltpu.make_async_copy(out_ref.at[half], out_hbm.at[:, pl.ds(half * LANES, LANES)], sems.at[half]))
+        copies[-1].start()
+    for copy in copies:
+        copy.wait()
 
 
 def shape32(*dims):
@@ -221,7 +229,6 @@
     _, tokens, channels = projections.shape
     mode_count = rates.shape[1]
     length = tokens // CHUNKS
-    grid = (channels // LANES,)
     halves = channels // LANES
     count = lax.axis_size("seq")
     index = lax.axis_index("seq")
@@ -258,17 +265,12 @@
         pltpu.with_memory_space_constraint(array, pltpu.HBM)
         for array in (rates.T, residues.T, taps, skip[None, :], projections)
     ))
-    taps_spec = by_lanes(3, tap_count)
-    modes_spec = by_lanes(mode_count)
-    grid_spec = by_lanes(length, CHUNKS)
-    ends_spec = by_lanes(mode_count, CHUNKS)
     local, gate = pl.pallas_call(
         local_kernel,
         out_shape=(shape32(length, CHUNKS, channels),) * 2,
-        grid=grid,
-        in_specs=[modes_spec, modes_spec, taps_spec, one_projection(0, tokens), grid_spec],
-        out_specs=(grid_spec, grid_spec),
-        scratch_shapes=[pltpu.VMEM((PAD + tokens, LANES), jnp.float32)],
+        in_specs=[vmem] * 5,
+        out_specs=(vmem, vmem),
+        scratch_shapes=[pltpu.VMEM((halves, PAD + tokens, LANES), jnp.float32)],
         compiler_params=PARAMS,
         name="local",
     )(rates_own, scale, taps, projections, gated)
@@ -320,6 +322,25 @@
         last = jnp.where(is_right, last, other_last)
         return (state, first, last), prefix, halo
 
+    def finish(kernel, prefix, halo, *earlier):
+        operands = (rates_own, scale, taps, skip, prefix, halo, head, ends, gated, local, gate)
+        return pl.pallas_call(
+            kernel,
+            out_shape=jax.ShapeDtypeStruct((tokens, channels), jnp.bfloat16),
+            in_specs=[vmem] * len(operands) + [hbm] * len(earlier),
+            out_specs=hbm,
+            scratch_shapes=[
+                pltpu.VMEM((3, 2 * PAD, LANES), jnp.float32),
+                pltpu.VMEM((halves, tokens, LANES), jnp.float32),
+                pltpu.VMEM((halves, tokens, LANES), jnp.bfloat16),
+                pltpu.SemaphoreType.DMA((halves,)),
+            ],
+            input_output_aliases={len(operands): 0} if earlier else {},
+            cost_estimate=pl.CostEstimate(flops=10_000_000, bytes_accessed=2_000_000, transcendentals=0),
+            compiler_params=PARAMS,
+            name="final",
+        )(*operands, *earlier)
+
     everyone, early, late = range(count), range(count // 2), range(count // 2, count)
     block, prefix, halo = (state, head[1:], tail), jnp.zeros_like(state), jnp.zeros_like(tail)
     block, prefix, halo = join(block, send(pack(*block), 1, everyone), prefix, halo, 1)
@@ -327,35 +348,24 @@
     received, local, gate = lax.optimization_barrier((received, local, gate))
     block, prefix, halo = join(block, received, prefix, halo, 2)
     packed = pack(*block)
-    received = send(packed, 5, early)
-    joined, _, _ = join(block, received, prefix, halo, 4)
+    received = lax.ppermute(packed, "seq", [(i, i ^ (5 if i in early else 1)) for i in everyone])
+    joined, early_prefix, early_halo = join(block, received, prefix, halo, 4)
+    out = finish(final_kernel, early_prefix, early_halo)
     total = pack(*joined)
     crossed = send(total, 13, early)
+    crossed, out = lax.optimization_barrier((crossed, out))
     left_state, _, left_last = unpack(crossed)
     offset = (index % (count // 2) * tokens).astype(jnp.float32)
     is_late = index >= count // 2
     prefix = prefix + jnp.where(is_late, decayed(offset), 0.0) * left_state
-    second, prefix, left_last = lax.optimization_barrier((send(packed, 5, late), prefix, left_last))
-    (_, first, _), prefix, halo = join(block, received + second, prefix, halo, 4)
+    second, prefix, left_last = lax.optimization_barrier(
+        (lax.ppermute(packed, "seq", [(i, i ^ (5 if i in late else 1)) for i in everyone]), prefix, left_last)
+    )
+    (_, first, _), prefix, halo = join(block, jnp.where(is_late, second, received), prefix, halo, 4)
     edge_part = decayed(jnp.maximum(offset - halo_rows, 0.0)) * edge_state_of(left_last, first)
     prefix = prefix + jnp.where(index > count // 2, edge_part, 0.0)
     halo = jnp.where(index == count // 2, left_last, halo)
-    return pl.pallas_call(
-        final_kernel,
-        out_shape=jax.ShapeDtypeStruct((tokens, channels), jnp.bfloat16),
-        grid=grid,
-        in_specs=[
-            modes_spec, modes_spec, taps_spec, by_lanes(1), modes_spec, by_lanes(3, PAD), by_lanes(3, PAD),
-            ends_spec, grid_spec, grid_spec, grid_spec,
-        ],
-        out_specs=by_lanes(tokens),
-        scratch_shapes=[
-            pltpu.VMEM((3, 2 * PAD, LANES), jnp.float32),
-            pltpu.VMEM((tokens, LANES), jnp.float32),
-        ],
-        compiler_params=PARAMS,
-        name="final",
-    )(rates_own, scale, taps, skip, prefix, halo, head, ends, gated, local, gate)
+    return finish(late_kernel, prefix, halo, out)
 
 
 def solution(mesh):

time: 22.9 us -> 21.3 us (0.930)
  starting transfers between devices: 8.9 us -> 8.06 us
  Pallas kernels: 6.16 us -> 5.78 us
  waiting for transfers between devices: 6.51 us -> 6.16 us
    ppermute x5 -> x3, waiting for transfers between devices: 6.51 us -> 2.58 us  [send(): return lax.ppermute(packed, 'seq', [(i, i ^ flip) for i in devices])]
    ppermute x0 -> x2, waiting for transfers between devices: none -> 3.58 us  [the longest x1 3.58 us: on_device(): lax.ppermute(packed, 'seq', [(i, i ^ (5 if i in early else 1)) for i in e...]
    ppermute x5 -> x3, starting transfers between devices: 8.9 us -> 6.25 us  [send(): return lax.ppermute(packed, 'seq', [(i, i ^ flip) for i in devices])]
    ppermute x0 -> x2, starting transfers between devices: none -> 1.81 us  [the longest x1 1.52 us: on_device(): lax.ppermute(packed, 'seq', [(i, i ^ (5 if i in early else 1)) for i in e...]
    pallas_call x1 -> x2, Pallas kernels: 1.82 us -> 1.64 us  [finish(): pl.pallas_call(kernel, out_shape=jax.ShapeDtypeStruct((tokens, channels),...]
  transfers between devices with their start and end apart: 5 -> 5, of which waited for: 4 -> 3; matrix products, arithmetic and copies ran while one was open for 0% -> 1% of each run, Pallas kernels for 8% -> 15%
where the time goes in v3:
time: 21.3 us; the launch traced here: 21.2 us
  starting transfers between devices  8.06 us (38%)
  waiting for transfers between devices  6.16 us (29%)
  Pallas kernels  5.78 us (27%)
  other arithmetic  0.61 us (3%)
  between operations  0.46 us (2%)
    ppermute x3, starting transfers between devices, send(): return lax.ppermute(packed, 'seq', [(i, i ^ flip) for i in devices])  6.25 us
    ppermute x1, waiting for transfers between devices, on_device(): lax.ppermute(packed, 'seq', [(i, i ^ (5 if i in early else 1)) for i in e...  3.58 us
    pallas_call x1, Pallas kernels, on_device(): pl.pallas_call(state_kernel, out_shape=(shape32(length, CHUNKS, channels)...  2.62 us
    ppermute x3, waiting for transfers between devices, send(): return lax.ppermute(packed, 'seq', [(i, i ^ flip) for i in devices])  2.58 us
    pallas_call x2, Pallas kernels, finish(): pl.pallas_call(kernel, out_shape=jax.ShapeDtypeStruct((tokens, channels),...  1.64 us
    ppermute x1, starting transfers between devices, on_device(): lax.ppermute(packed, 'seq', [(i, i ^ (5 if i in early else 1)) for i in e...  1.52 us
    pallas_call x1, Pallas kernels, on_device(): pl.pallas_call(local_kernel, out_shape=(shape32(length, CHUNKS, channels)...  1.51 us
  transfers between devices with their start and end apart: 5, of which 3 were waited for; matrix products, arithmetic and copies ran while one was open for 1% of the time, Pallas kernels for 15%

profile of v3, /device:TPU:1, one launch (start us, length us, event | category | flops | bytes accessed | tf_op | source)
XLA Modules:
  0.0 21.2 jit_solution(2471070852245599255)
XLA Ops:
  0.0 2.6 %state.1 = (f32[64,8,256]{2,1,0:T(8,128)S(1)}, f32[16,8,256]{2,1,0:T(8,128)S(1)}, f32[16,256]{1,0:T(8,128)S(1)}, f32[3,8,256]{2,1,0:T(8,128)S(1)}, f32[3,8,256]{...) custom-call(f32[16,4096]{1,0:T(8,128)} %bitcast.123, ...), custom_call_target="tpu_custom_call" | custom-call | tf_op jit(solution)/shard_map/state/pallas_call | solution.py:238
  2.6 0.0 copy-start
  2.7 3.3 %collective-permute-start = (bf16[72,256]{1,0:T(8,128)(2,1)S(1)}, bf16[72,256]{1,0:T(8,128)(2,1)S(1)}, u32[]{:S(2)}, u32[]{:S(2)}) collective-permute-start(bf16[72,256]{1,0:T(8,128)(2,1)S(1)} %pad_maximum_fusion), channel_id=1, source_target_pairs={{0,16},{16,0},{32,48},{48,32},{64,80},{80,64},{96,112},{112,96},{1... | collective-permute-start | bytes 110600 | tf_op jit(solution)/shard_map/ppermute | solution.py:292
  6.1 0.8 %collective-permute-done = bf16[72,256]{1,0:T(8,128)(2,1)S(1)} collective-permute-done((bf16[72,256]{1,0:T(8,128)(2,1)S(1)}, bf16[72,256]{1,0:T(8,128)(2,1)S(1)}, u32[]{:S(2)}, u32[]{:S(2)}) %collective-permute-start) | collective-permute-done | bytes 36896 | tf_op jit(solution)/shard_map/ppermute | solution.py:292
  7.1 0.2 %collective-permute-start.1 = (bf16[72,256]{1,0:T(8,128)(2,1)S(1)}, bf16[72,256]{1,0:T(8,128)(2,1)S(1)}, u32[]{:S(2)}, u32[]{:S(2)}) collective-permute-start(bf16[72,256]{1,0:T(8,128)(2,1)S(1)} %pad_maximum_fusion.1), channel_id=1, source_target_pairs={{0,48},{16,32},{32,16},{48,0},{64,112},{80,96},{96,80},{112,64},{1... | collective-permute-start | bytes 110600 | tf_op jit(solution)/shard_map/ppermute | solution.py:292
  7.3 0.0 copy-done
  7.3 1.5 %local.1 = (f32[64,8,256]{2,1,0:T(8,128)S(1)}, f32[64,8,256]{2,1,0:T(8,128)S(1)}) custom-call(f32[16,256]{1,0:T(8,128)S(1)} %get-tuple-element.24.rates_ref.refs_0_, f32[16,256]{1,0:T(8,128)S(1)} %get-tuple-element.25.scale_ref.refs_1_, f32[3,7,256]{2,1,0:T(8,128)S(1)} %get-tuple-element.26.taps_ref.refs_2_, bf16[3,512,256]{2,1,0:T(8,128)(2,1)S(1)} %copy-done, ...), custom_call_target="tpu_custom_call" | custom-call | tf_op jit(solution)/shard_map/local/pallas_call | solution.py:268
  8.8 1.8 %collective-permute-done.1 = bf16[72,256]{1,0:T(8,128)(2,1)S(1)} collective-permute-done((bf16[72,256]{1,0:T(8,128)(2,1)S(1)}, bf16[72,256]{1,0:T(8,128)(2,1)S(1)}, u32[]{:S(2)}, u32[]{:S(2)}) %collective-permute-start.1) | collective-permute-done | bytes 36896 | tf_op jit(solution)/shard_map/ppermute | solution.py:292
  10.8 1.5 %collective-permute-start.3 = (bf16[72,256]{1,0:T(8,128)(2,1)S(1)}, bf16[72,256]{1,0:T(8,128)(2,1)S(1)}, u32[]{:S(2)}, u32[]{:S(2)}) collective-permute-start(bf16[72,256]{1,0:T(8,128)(2,1)S(1)} %pad_maximum_fusion.2), channel_id=1, source_target_pairs={{0,80},{16,64},{32,112},{48,96},{64,16},{80,0},{96,48},{112,32},{1... | collective-permute-start | bytes 110600 | tf_op jit(solution)/shard_map/ppermute | solution.py:351
  12.3 0.3 %collective-permute-start.2 = (bf16[72,256]{1,0:T(8,128)(2,1)S(1)}, bf16[72,256]{1,0:T(8,128)(2,1)S(1)}, u32[]{:S(2)}, u32[]{:S(2)}) collective-permute-start(bf16[72,256]{1,0:T(8,128)(2,1)S(1)} %pad_maximum_fusion.2), channel_id=1, source_target_pairs={{0,16},{16,0},{32,48},{48,32},{64,80},{80,64},{96,112},{112,96},{1... | collective-permute-start | bytes 110600 | tf_op jit(solution)/shard_map/ppermute | solution.py:362
  12.6 3.6 %collective-permute-done.3 = bf16[72,256]{1,0:T(8,128)(2,1)S(1)} collective-permute-done((bf16[72,256]{1,0:T(8,128)(2,1)S(1)}, bf16[72,256]{1,0:T(8,128)(2,1)S(1)}, u32[]{:S(2)}, u32[]{:S(2)}) %collective-permute-start.3) | collective-permute-done | bytes 36896 | tf_op jit(solution)/shard_map/ppermute | solution.py:351
  16.4 2.7 %collective-permute-start.4 = (bf16[72,256]{1,0:T(8,128)(2,1)S(1)}, bf16[72,256]{1,0:T(8,128)(2,1)S(1)}, u32[]{:S(2)}, u32[]{:S(2)}) collective-permute-start(bf16[72,256]{1,0:T(8,128)(2,1)S(1)} %pad_maximum_fusion.3), channel_id=1, source_target_pairs={{0,208},{16,192},{32,240},{48,224},{64,144},{80,128},{96,176},{112... | collective-permute-start | bytes 110600 | tf_op jit(solution)/shard_map/ppermute | solution.py:292
  19.1 0.1 add_select_fusion.1
  19.2 1.6 %final.2.refs_11_ = bf16[512,256]{1,0:T(8,128)(2,1)} custom-call(f32[16,256]{1,0:T(8,128)S(1)} %get-tuple-element.24.rates_ref.refs_0_, f32[16,256]{1,0:T(8,128)S(1)} %get-tuple-element.25.scale_ref.refs_1_, f32[3,7,256]{2,1,0:T(8,128)S(1)} %get-tuple-element.26.taps_ref.refs_2_, f32[1,256]{1,0:T(1,128)S(1)} %get-tuple-element.27.skip_ref.refs_3_, ...), custom_call_target="tpu_custom_call" | custom-call | flops 10000000 | bytes 2000000 | tf_op jit(solution)/shard_map/final/pallas_call | solution.py:327
  20.8 0.0 collective-permute-done.4
  20.9 0.0 collective-permute-done.2
  20.9 0.1 fusion.24
  (58 shorter events, 0.6 us)
Async XLA Ops:
  2.6 4.7 %copy-start = (bf16[3,512,256]{2,1,0:T(8,128)(2,1)S(1)}, bf16[3,512,256]{2,1,0:T(8,128)(2,1)}, u32[]{:S(2)}) copy-start(bf16[3,512,256]{2,1,0:T(8,128)(2,1)} %tokens_ref.1) | copy-start | bytes 2359300
  2.7 4.2 %collective-permute-start = (bf16[72,256]{1,0:T(8,128)(2,1)S(1)}, bf16[72,256]{1,0:T(8,128)(2,1)S(1)}, u32[]{:S(2)}, u32[]{:S(2)}) collective-permute-start(bf16[72,256]{1,0:T(8,128)(2,1)S(1)} %pad_maximum_fusion), channel_id=1, source_target_pairs={{0,16},{16,0},{32,48},{48,32},{64,80},{80,64},{96,112},{112,96},{1... | collective-permute-start | bytes 110600 | tf_op jit(solution)/shard_map/ppermute | solution.py:292
  7.1 3.5 %collective-permute-start.1 = (bf16[72,256]{1,0:T(8,128)(2,1)S(1)}, bf16[72,256]{1,0:T(8,128)(2,1)S(1)}, u32[]{:S(2)}, u32[]{:S(2)}) collective-permute-start(bf16[72,256]{1,0:T(8,128)(2,1)S(1)} %pad_maximum_fusion.1), channel_id=1, source_target_pairs={{0,48},{16,32},{32,16},{48,0},{64,112},{80,96},{96,80},{112,64},{1... | collective-permute-start | bytes 110600 | tf_op jit(solution)/shard_map/ppermute | solution.py:292
  10.8 5.4 %collective-permute-start.3 = (bf16[72,256]{1,0:T(8,128)(2,1)S(1)}, bf16[72,256]{1,0:T(8,128)(2,1)S(1)}, u32[]{:S(2)}, u32[]{:S(2)}) collective-permute-start(bf16[72,256]{1,0:T(8,128)(2,1)S(1)} %pad_maximum_fusion.2), channel_id=1, source_target_pairs={{0,80},{16,64},{32,112},{48,96},{64,16},{80,0},{96,48},{112,32},{1... | collective-permute-start | bytes 110600 | tf_op jit(solution)/shard_map/ppermute | solution.py:351
  12.3 8.6 %collective-permute-start.2 = (bf16[72,256]{1,0:T(8,128)(2,1)S(1)}, bf16[72,256]{1,0:T(8,128)(2,1)S(1)}, u32[]{:S(2)}, u32[]{:S(2)}) collective-permute-start(bf16[72,256]{1,0:T(8,128)(2,1)S(1)} %pad_maximum_fusion.2), channel_id=1, source_target_pairs={{0,16},{16,0},{32,48},{48,32},{64,80},{80,64},{96,112},{112,96},{1... | collective-permute-start | bytes 110600 | tf_op jit(solution)/shard_map/ppermute | solution.py:362
  16.4 4.4 %collective-permute-start.4 = (bf16[72,256]{1,0:T(8,128)(2,1)S(1)}, bf16[72,256]{1,0:T(8,128)(2,1)S(1)}, u32[]{:S(2)}, u32[]{:S(2)}) collective-permute-start(bf16[72,256]{1,0:T(8,128)(2,1)S(1)} %pad_maximum_fusion.3), channel_id=1, source_target_pairs={{0,208},{16,192},{32,240},{48,224},{64,144},{80,128},{96,176},{112... | collective-permute-start | bytes 110600 | tf_op jit(solution)/shard_map/ppermute | solution.py:292

commit v4 on v3

--- a/solution.py
+++ b/solution.py
@@ -6,6 +6,7 @@
 from jax.sharding import PartitionSpec as P
 
 CHUNKS = 8
+CROSSING = {0: 12, 1: 15, 2: 14, 3: 13, 4: 9, 5: 8, 6: 11, 7: 10}
 LANES = 128
 PAD = 8
 
@@ -280,13 +281,17 @@
 
     def pack(state, first, last):
         high = lax.reduce_precision(state, 8, 7)
-        rows = [high, state - high, last.reshape(3 * PAD, channels), first.reshape(2 * PAD, channels)]
+        rows = [high, state - high, last[:, PAD - halo_rows :].reshape(3 * halo_rows, channels)]
+        if first is not None:
+            rows.append(first[:, :halo_rows].reshape(2 * halo_rows, channels))
         return jnp.concatenate(rows, axis=0).astype(jnp.bfloat16)
 
     def unpack(packed):
         packed = packed.astype(jnp.float32)
-        edges = packed[2 * mode_count :].reshape(5, PAD, channels)
-        return packed[:mode_count] + packed[mode_count : 2 * mode_count], edges[3:], edges[:3]
+        edges = packed[2 * mode_count :].reshape(-1, halo_rows, channels)
+        last = jnp.pad(edges[:3], ((0, 0), (PAD - halo_rows, 0), (0, 0)))
+        first = jnp.pad(edges[3:], ((0, 0), (0, PAD - halo_rows), (0, 0)))
+        return packed[:mode_count] + packed[mode_count : 2 * mode_count], first, last
 
     def send(packed, flip, devices):
         return lax.ppermute(packed, "seq", [(i, i ^ flip) for i in devices])
@@ -351,8 +356,8 @@
     received = lax.ppermute(packed, "seq", [(i, i ^ (5 if i in early else 1)) for i in everyone])
     joined, early_prefix, early_halo = join(block, received, prefix, halo, 4)
     out = finish(final_kernel, early_prefix, early_halo)
-    total = pack(*joined)
-    crossed = send(total, 13, early)
+    total = pack(joined[0], None, joined[2])
+    crossed = lax.ppermute(total, "seq", list(CROSSING.items()))
     crossed, out = lax.optimization_barrier((crossed, out))
     left_state, _, left_last = unpack(crossed)
     offset = (index % (count // 2) * tokens).astype(jnp.float32)

time: 21.3 us -> 20.9 us (0.981)
  starting transfers between devices: 8.06 us -> 7.61 us
  waiting for transfers between devices: 6.16 us -> 5.86 us
    ppermute x3 -> x2, starting transfers between devices: 6.25 us -> 3.56 us  [send(): return lax.ppermute(packed, 'seq', [(i, i ^ flip) for i in devices])]
    ppermute x0 -> x1, starting transfers between devices: none -> 2.2 us  [on_device(): crossed = lax.ppermute(total, 'seq', list(CROSSING.items()))]
    ppermute x3 -> x2, waiting for transfers between devices: 2.58 us -> 2.48 us  [send(): return lax.ppermute(packed, 'seq', [(i, i ^ flip) for i in devices])]
  transfers between devices with their start and end apart: 5 -> 5, of which waited for: 3 -> 3; matrix products, arithmetic and copies ran while one was open for 1% -> 2% of each run, Pallas kernels for 15% -> 15%
where the time goes in v4:
time: 20.9 us; the launch traced here: 20.8 us
  starting transfers between devices  7.61 us (36%)
  waiting for transfers between devices  5.86 us (28%)
  Pallas kernels  5.78 us (28%)
  other arithmetic  0.65 us (3%)
  between operations  0.62 us (3%)
  local copies, waits for them, and re-layouts  0.26 us (1%)
    ppermute x2, starting transfers between devices, send(): return lax.ppermute(packed, 'seq', [(i, i ^ flip) for i in devices])  3.56 us
    ppermute x1, waiting for transfers between devices, on_device(): lax.ppermute(packed, 'seq', [(i, i ^ (5 if i in early else 1)) for i in e...  3.37 us
    pallas_call x1, Pallas kernels, on_device(): pl.pallas_call(state_kernel, out_shape=(shape32(length, CHUNKS, channels)...  2.62 us
    ppermute x2, waiting for transfers between devices, send(): return lax.ppermute(packed, 'seq', [(i, i ^ flip) for i in devices])  2.48 us
    ppermute x1, starting transfers between devices, on_device(): crossed = lax.ppermute(total, 'seq', list(CROSSING.items()))  2.2 us
    pallas_call x2, Pallas kernels, finish(): pl.pallas_call(kernel, out_shape=jax.ShapeDtypeStruct((tokens, channels),...  1.64 us
    ppermute x1, starting transfers between devices, on_device(): lax.ppermute(packed, 'seq', [(i, i ^ (5 if i in early else 1)) for i in e...  1.56 us
    pallas_call x1, Pallas kernels, on_device(): pl.pallas_call(local_kernel, out_shape=(shape32(length, CHUNKS, channels)...  1.51 us
  transfers between devices with their start and end apart: 5, of which 3 were waited for; matrix products, arithmetic and copies ran while one was open for 2% of the time, Pallas kernels for 15%

profile of v4, /device:TPU:1, one launch (start us, length us, event | category | flops | bytes accessed | tf_op | source)
XLA Modules:
  0.0 20.8 jit_solution(1471906837727318682)
XLA Ops:
  0.0 2.6 %state.1 = (f32[64,8,256]{2,1,0:T(8,128)S(1)}, f32[16,8,256]{2,1,0:T(8,128)S(1)}, f32[16,256]{1,0:T(8,128)S(1)}, f32[3,8,256]{2,1,0:T(8,128)S(1)}, f32[3,8,256]{...) custom-call(f32[16,4096]{1,0:T(8,128)} %bitcast.49, ...), custom_call_target="tpu_custom_call" | custom-call | tf_op jit(solution)/shard_map/state/pallas_call | solution.py:239
  2.6 0.0 copy-start
  2.7 3.3 %collective-permute-start = (bf16[62,256]{1,0:T(8,128)(2,1)S(1)}, bf16[62,256]{1,0:T(8,128)(2,1)S(1)}, u32[]{:S(2)}, u32[]{:S(2)}) collective-permute-start(bf16[62,256]{1,0:T(8,128)(2,1)S(1)} %pad_maximum_fusion), channel_id=1, source_target_pairs={{0,16},{16,0},{32,48},{48,32},{64,80},{80,64},{96,112},{112,96},{1... | collective-permute-start | bytes 95240 | tf_op jit(solution)/shard_map/ppermute | solution.py:297
  6.1 0.8 %collective-permute-done = bf16[62,256]{1,0:T(8,128)(2,1)S(1)} collective-permute-done((bf16[62,256]{1,0:T(8,128)(2,1)S(1)}, bf16[62,256]{1,0:T(8,128)(2,1)S(1)}, u32[]{:S(2)}, u32[]{:S(2)}) %collective-permute-start) | collective-permute-done | bytes 31776 | tf_op jit(solution)/shard_map/ppermute | solution.py:297
  7.2 0.2 %collective-permute-start.1 = (bf16[62,256]{1,0:T(8,128)(2,1)S(1)}, bf16[62,256]{1,0:T(8,128)(2,1)S(1)}, u32[]{:S(2)}, u32[]{:S(2)}) collective-permute-start(bf16[62,256]{1,0:T(8,128)(2,1)S(1)} %pad_maximum_fusion.1), channel_id=1, source_target_pairs={{0,48},{16,32},{32,16},{48,0},{64,112},{80,96},{96,80},{112,64},{1... | collective-permute-start | bytes 95240 | tf_op jit(solution)/shard_map/ppermute | solution.py:297
  7.4 0.0 copy-done
  7.4 1.5 %local.1 = (f32[64,8,256]{2,1,0:T(8,128)S(1)}, f32[64,8,256]{2,1,0:T(8,128)S(1)}) custom-call(f32[16,256]{1,0:T(8,128)S(1)} %get-tuple-element.24.rates_ref.refs_0_, f32[16,256]{1,0:T(8,128)S(1)} %get-tuple-element.25.scale_ref.refs_1_, f32[3,7,256]{2,1,0:T(8,128)S(1)} %get-tuple-element.26.taps_ref.refs_2_, bf16[3,512,256]{2,1,0:T(8,128)(2,1)S(1)} %copy-done, ...), custom_call_target="tpu_custom_call" | custom-call | tf_op jit(solution)/shard_map/local/pallas_call | solution.py:269
  8.9 1.7 %collective-permute-done.1 = bf16[62,256]{1,0:T(8,128)(2,1)S(1)} collective-permute-done((bf16[62,256]{1,0:T(8,128)(2,1)S(1)}, bf16[62,256]{1,0:T(8,128)(2,1)S(1)}, u32[]{:S(2)}, u32[]{:S(2)}) %collective-permute-start.1) | collective-permute-done | bytes 31776 | tf_op jit(solution)/shard_map/ppermute | solution.py:297
  10.9 1.6 %collective-permute-start.3 = (bf16[62,256]{1,0:T(8,128)(2,1)S(1)}, bf16[62,256]{1,0:T(8,128)(2,1)S(1)}, u32[]{:S(2)}, u32[]{:S(2)}) collective-permute-start(bf16[62,256]{1,0:T(8,128)(2,1)S(1)} %pad_maximum_fusion.2), channel_id=1, source_target_pairs={{0,80},{16,64},{32,112},{48,96},{64,16},{80,0},{96,48},{112,32},{1... | collective-permute-start | bytes 95240 | tf_op jit(solution)/shard_map/ppermute | solution.py:356
  12.5 0.3 %collective-permute-start.2 = (bf16[62,256]{1,0:T(8,128)(2,1)S(1)}, bf16[62,256]{1,0:T(8,128)(2,1)S(1)}, u32[]{:S(2)}, u32[]{:S(2)}) collective-permute-start(bf16[62,256]{1,0:T(8,128)(2,1)S(1)} %pad_maximum_fusion.2), channel_id=1, source_target_pairs={{0,16},{16,0},{32,48},{48,32},{64,80},{80,64},{96,112},{112,96},{1... | collective-permute-start | bytes 95240 | tf_op jit(solution)/shard_map/ppermute | solution.py:367
  12.8 3.4 %collective-permute-done.3 = bf16[62,256]{1,0:T(8,128)(2,1)S(1)} collective-permute-done((bf16[62,256]{1,0:T(8,128)(2,1)S(1)}, bf16[62,256]{1,0:T(8,128)(2,1)S(1)}, u32[]{:S(2)}, u32[]{:S(2)}) %collective-permute-start.3) | collective-permute-done | bytes 31776 | tf_op jit(solution)/shard_map/ppermute | solution.py:356
  16.4 2.2 %collective-permute-start.4 = (bf16[50,256]{1,0:T(8,128)(2,1)S(1)}, bf16[50,256]{1,0:T(8,128)(2,1)S(1)}, u32[]{:S(2)}, u32[]{:S(2)}) collective-permute-start(bf16[50,256]{1,0:T(8,128)(2,1)S(1)} %pad_maximum_fusion.3), channel_id=1, source_target_pairs={{0,192},{16,240},{32,224},{48,208},{64,144},{80,128},{96,176},{112... | collective-permute-start | bytes 76808 | tf_op jit(solution)/shard_map/ppermute | solution.py:360
  18.6 0.1 add_select_fusion.1
  18.7 1.6 %final.2.refs_11_ = bf16[512,256]{1,0:T(8,128)(2,1)} custom-call(f32[16,256]{1,0:T(8,128)S(1)} %get-tuple-element.24.rates_ref.refs_0_, f32[16,256]{1,0:T(8,128)S(1)} %get-tuple-element.25.scale_ref.refs_1_, f32[3,7,256]{2,1,0:T(8,128)S(1)} %get-tuple-element.26.taps_ref.refs_2_, f32[1,256]{1,0:T(1,128)S(1)} %get-tuple-element.27.skip_ref.refs_3_, ...), custom_call_target="tpu_custom_call" | custom-call | flops 10000000 | bytes 2000000 | tf_op jit(solution)/shard_map/final/pallas_call | solution.py:332
  20.3 0.0 collective-permute-done.4
  20.4 0.0 collective-permute-done.2
  20.6 0.1 fusion.25
  (82 shorter events, 0.8 us)
Async XLA Ops:
  2.6 4.8 %copy-start = (bf16[3,512,256]{2,1,0:T(8,128)(2,1)S(1)}, bf16[3,512,256]{2,1,0:T(8,128)(2,1)}, u32[]{:S(2)}) copy-start(bf16[3,512,256]{2,1,0:T(8,128)(2,1)} %tokens_ref.1) | copy-start | bytes 2359300
  2.7 4.2 %collective-permute-start = (bf16[62,256]{1,0:T(8,128)(2,1)S(1)}, bf16[62,256]{1,0:T(8,128)(2,1)S(1)}, u32[]{:S(2)}, u32[]{:S(2)}) collective-permute-start(bf16[62,256]{1,0:T(8,128)(2,1)S(1)} %pad_maximum_fusion), channel_id=1, source_target_pairs={{0,16},{16,0},{32,48},{48,32},{64,80},{80,64},{96,112},{112,96},{1... | collective-permute-start | bytes 95240 | tf_op jit(solution)/shard_map/ppermute | solution.py:297
  7.2 3.4 %collective-permute-start.1 = (bf16[62,256]{1,0:T(8,128)(2,1)S(1)}, bf16[62,256]{1,0:T(8,128)(2,1)S(1)}, u32[]{:S(2)}, u32[]{:S(2)}) collective-permute-start(bf16[62,256]{1,0:T(8,128)(2,1)S(1)} %pad_maximum_fusion.1), channel_id=1, source_target_pairs={{0,48},{16,32},{32,16},{48,0},{64,112},{80,96},{96,80},{112,64},{1... | collective-permute-start | bytes 95240 | tf_op jit(solution)/shard_map/ppermute | solution.py:297
  10.9 5.2 %collective-permute-start.3 = (bf16[62,256]{1,0:T(8,128)(2,1)S(1)}, bf16[62,256]{1,0:T(8,128)(2,1)S(1)}, u32[]{:S(2)}, u32[]{:S(2)}) collective-permute-start(bf16[62,256]{1,0:T(8,128)(2,1)S(1)} %pad_maximum_fusion.2), channel_id=1, source_target_pairs={{0,80},{16,64},{32,112},{48,96},{64,16},{80,0},{96,48},{112,32},{1... | collective-permute-start | bytes 95240 | tf_op jit(solution)/shard_map/ppermute | solution.py:356
  12.5 7.9 %collective-permute-start.2 = (bf16[62,256]{1,0:T(8,128)(2,1)S(1)}, bf16[62,256]{1,0:T(8,128)(2,1)S(1)}, u32[]{:S(2)}, u32[]{:S(2)}) collective-permute-start(bf16[62,256]{1,0:T(8,128)(2,1)S(1)} %pad_maximum_fusion.2), channel_id=1, source_target_pairs={{0,16},{16,0},{32,48},{48,32},{64,80},{80,64},{96,112},{112,96},{1... | collective-permute-start | bytes 95240 | tf_op jit(solution)/shard_map/ppermute | solution.py:367
  16.4 3.9 %collective-permute-start.4 = (bf16[50,256]{1,0:T(8,128)(2,1)S(1)}, bf16[50,256]{1,0:T(8,128)(2,1)S(1)}, u32[]{:S(2)}, u32[]{:S(2)}) collective-permute-start(bf16[50,256]{1,0:T(8,128)(2,1)S(1)} %pad_maximum_fusion.3), channel_id=1, source_target_pairs={{0,192},{16,240},{32,224},{48,208},{64,144},{80,128},{96,176},{112... | collective-permute-start | bytes 76808 | tf_op jit(solution)/shard_map/ppermute | solution.py:360
